TPU v7x, 128 devices: a whole 4x4x4 slice. The times are simulated.
128 devices in a mesh: grp: 4 (over z_lo, core), kp: 32 (over x, z_hi, y).
Axes of the slice: x: 4, y: 4, z: 4 (z_hi: 2, z_lo: 2; z = z_hi * 2 + z_lo), core: 2. Of those that a mesh axis runs over, the one named last changes fastest.
Arguments:
- g_real: bfloat16 [2, 1024, 6144], P(None, 'kp'), may hold values from -0.1875 to 0.1875
- lattice: int32 [3, 1024], replicated, may hold values from -20 to 20
- u_rot: float32 [2, 16, 16, 16384], P(None, None, None, ('grp', 'kp')), may hold values from -1.5 to 1.5
- energy: float32 [16, 16384], P(None, ('grp', 'kp')), may hold values from -2 to 2
- band_mask: int32 [16, 16384], P(None, ('grp', 'kp')), may hold values 0 or 1
- freq: float32 [2, 12], replicated, may hold values from 0.01 to 0.1
- froh: float32 [2, 2, 12], replicated, may hold values from -6 to 6
- kq_index: int32 [2, 128], replicated, may hold values from 0 to 127, each once within a row
- irr_id: int32 [16384], P(('grp', 'kp')), may hold values from 0 to 511
Outputs:
- sigma_k: float32 [2, 16, 16384], P(None, None, ('grp', 'kp'))
- sigma_irr: float32 [2, 16, 2048], P(None, None, ('grp', 'kp'))
Inputs may be any that keep to these rules, and one draw needn't show every extreme that they name: `kq_index`: each row is a permutation of the positions 0 to 127. `irr_id`: irreducible points are numbered within a block of 4096 k points.
All inputs are finite; a program needn't handle non-finite values. No bound on the sum of `band_mask` on one device may be relied on, other than what follows from the above.
Results may differ from a plain program's by a relative error of at most 0.0027.
Values may be sent and summed in bfloat16 or wider, within the bound.
A program may use at most 192 MiB of HBM per device.

v0:
```python
import math

import jax
import jax.numpy as jnp
from jax import lax
from jax.sharding import PartitionSpec as P

NKM = 40
IRR_DEV = 16


KT = 0.025
ETA = 0.05
TWO_PI = 2.0 * math.pi


def shifted(array, axis, by):
    size = lax.axis_size(axis)
    return lax.ppermute(array, axis, [(i, (i + by) % size) for i in range(size)])


def grid_points(first, count):
    index = first + jnp.arange(count, dtype=jnp.int32)
    return (index % NKM, index // NKM % NKM, index // (NKM * NKM) % NKM)


def phase_matrix(lattice_cols, grid):
    turns = (
        lattice_cols[0][:, None] * grid[0][None, :] + lattice_cols[1][:, None] * grid[1][None, :]
    )
    turns = jnp.mod(turns + lattice_cols[2][:, None] * grid[2][None, :], NKM)
    angle = turns.astype(jnp.float32) * (TWO_PI / NKM)
    cosine = jnp.cos(angle).astype(jnp.bfloat16)
    sine = jnp.sin(angle).astype(jnp.bfloat16)
    return jnp.stack([jnp.concatenate([cosine, sine], 1), jnp.concatenate([-sine, cosine], 1)])


def fourier(rows, phases):
    split = rows.reshape(rows.shape[0], 2, rows.shape[1] // 2)
    return lax.dot_general(
        split, phases, (((0, 1), (1, 0)), ((), ())), preferred_element_type=jnp.float32
    )


def contribution(vertex, own_rot, own_energy, far_rot, far_extra, freq_row, froh_row):
    modes = freq_row.shape[0]
    width = own_rot.shape[1]
    count = own_rot.shape[3]
    vertex_re = vertex[:, :count].reshape(modes, width, width, count)
    vertex_im = vertex[:, count:].reshape(modes, width, width, count)
    own_re, own_im = (own_rot[0], own_rot[1])
    far_re, far_im = (far_rot[0], far_rot[1])
    coup_re = froh_row[0][:, None, None, None]
    coup_im = froh_row[1][:, None, None, None]
    mixed_re = coup_re * own_re[None] - coup_im * own_im[None]
    mixed_im = coup_re * own_im[None] + coup_im * own_re[None]
    for inner in range(width):
        left_re = vertex_re[:, :, inner][:, :, None, :]
        left_im = vertex_im[:, :, inner][:, :, None, :]
        right_re = own_re[inner][None, None]
        right_im = own_im[inner][None, None]
        mixed_re = mixed_re + left_re * right_re - left_im * right_im
        mixed_im = mixed_im + left_re * right_im + left_im * right_re
    bloch_re = jnp.zeros((modes, width, width, count), jnp.float32)
    bloch_im = jnp.zeros((modes, width, width, count), jnp.float32)
    for inner in range(width):
        rot_re = far_re[inner][None, :, None, :]
        rot_im = far_im[inner][None, :, None, :]
        part_re = mixed_re[:, inner][:, None]
        part_im = mixed_im[:, inner][:, None]
        bloch_re = bloch_re + rot_re * part_re + rot_im * part_im
        bloch_im = bloch_im + rot_re * part_im - rot_im * part_re
    strength = (bloch_re * bloch_re + bloch_im * bloch_im) * far_extra[1][None, :, None, :]
    far_energy = far_extra[0]
    occupied = (1.0 / (jnp.exp(far_energy / KT) + 1.0))[None, :, None, :]
    bose = (1.0 / (jnp.exp(freq_row / KT) - 1.0))[:, None, None, None]
    phonon = freq_row[:, None, None, None]
    differ = own_energy[None, None, :, :] - far_energy[None, :, None, :]
    upper = differ + phonon
    lower = differ - phonon
    denom_up = upper * upper + ETA * ETA
    denom_low = lower * lower + ETA * ETA
    emission = bose + occupied
    absorb = bose + 1.0 - occupied
    real_part = strength * (emission * upper / denom_up + absorb * lower / denom_low)
    imag_part = -ETA * strength * (emission / denom_up + absorb / denom_low)
    return jnp.stack([real_part.sum((0, 1)), imag_part.sum((0, 1))])


def local(g_real, lattice, u_rot, energy, band_mask, freq, froh, kq_index, irr_id):
    count = u_rot.shape[3]
    width = u_rot.shape[1]
    steps = g_real.shape[0]
    members = lax.axis_size("kp")
    first = (lax.axis_index("grp") * members + lax.axis_index("kp")) * count
    grid = grid_points(first, count)
    extra = jnp.stack([energy, band_mask.astype(jnp.float32)])
    weight = 1.0 / (steps * freq.shape[1] * width)
    gathered = lax.all_gather(g_real, "kp", axis=1, tiled=True)
    phases = phase_matrix(lattice, grid)
    total = jnp.zeros((2, width, count), jnp.float32)
    for step in range(steps):
        vertex = fourier(gathered[step], phases)
        far_rot, far_extra = shifted((u_rot, extra), "grp", -(step + 1))
        order = kq_index[step]
        far_rot = jnp.take(far_rot, order, axis=3)
        far_extra = jnp.take(far_extra, order, axis=2)
        total = total + contribution(
            vertex, u_rot, energy, far_rot, far_extra, freq[step], froh[step]
        )
    sigma_k = total * weight
    flat = sigma_k.reshape(2 * width, count)
    labels = jnp.arange(IRR_DEV * members, dtype=jnp.int32)
    member = (labels[:, None] == irr_id[None, :]).astype(jnp.float32)
    partial_sums = lax.dot_general(
        member,
        flat,
        (((1,), (1,)), ((), ())),
        precision=lax.Precision.HIGHEST,
        preferred_element_type=jnp.float32,
    )
    tallies = member.sum(1)
    owned, tally = (
        lax.psum_scatter(partial_sums, "kp", scatter_dimension=0, tiled=True),
        lax.psum_scatter(tallies, "kp", scatter_dimension=0, tiled=True),
    )
    summed = owned.T
    sigma_irr = (summed / jnp.maximum(tally, 1.0)[None, :]).reshape(2, width, IRR_DEV)
    return (sigma_k, sigma_irr)


def solution(mesh):
    in_specs = (
        P(None, "kp", None),
        P(),
        P(None, None, None, ("grp", "kp")),
        P(None, ("grp", "kp")),
        P(None, ("grp", "kp")),
        P(),
        P(),
        P(),
        P(("grp", "kp")),
    )
    out_specs = (P(None, None, ("grp", "kp")), P(None, None, ("grp", "kp")))
    return jax.shard_map(local, mesh=mesh, in_specs=in_specs, out_specs=out_specs, check_vma=False)
```

profile of v0, /device:TPU:0, one launch (start us, length us, event | category | flops | bytes accessed | tf_op | source)
XLA Modules:
  0.0 642.7 jit_solution(9284518485056793770)
XLA Ops:
  7.3 2.9 copy.523
  10.4 2.1 collective-permute-start.3
  12.5 1.2 collective-permute-start.2
  14.7 2.3 fusion.36
  17.1 2.5 sine_convert_fusion
  28.4 1.8 copy.593
  30.2 2.2 gather_fusion.2
  33.4 2.1 gather_fusion
  35.5 2.6 select_bitcast_fusion
  38.1 1.4 copy-done
  39.5 1.8 fusion.42
  41.2 1.5 copy.590
  42.7 1.5 copy.589
  44.3 1.5 copy.588
  45.8 1.5 copy.587
  47.3 1.5 copy.586
  48.8 1.5 copy.585
  50.3 1.5 copy.584
  51.8 1.5 copy.583
  53.3 1.5 copy.582
  60.8 5.5 fusion.43
  66.3 1.5 copy.572
  67.8 1.5 copy.571
  69.3 1.5 copy.570
  70.8 1.5 copy.569
  78.9 1.8 fusion.40
  80.7 1.5 copy.661
  82.2 1.5 copy.660
  83.7 1.5 copy.659
  85.2 1.5 copy.658
  86.7 1.5 copy.657
  88.2 1.5 copy.656
  89.7 1.5 copy.655
  91.2 1.5 copy.654
  92.7 1.5 copy.653
  100.2 1.4 fusion.41
  101.6 1.5 copy.643
  103.1 1.5 copy.642
  104.6 1.5 copy.641
  106.1 1.5 copy.640
  114.3 108.0 %all-gather.2.cloned.1.call-done = bf16[2,1024,6144]{2,0,1:T(2,128)(2,1)} async-done(((bf16[2,32,6144]{2,0,1:T(2,128)(2,1)}), bf16[2,1024,6144]{2,0,1:T(2,128)(2,1)}) %all-gather.2.cloned.1.call-update) | async-done | bytes 25165840 | tf_op jit(solution)/shard_map/all_gather | solution.py:99
  222.3 47.1 %fusion.37 = (bf16[1,1024,6144]{2,0,1:T(2,128)(2,1)}, bf16[1,1024,6144]{2,0,1:T(2,128)(2,1)}) fusion(bf16[2,1024,6144]{2,0,1:T(2,128)(2,1)} %all-gather.2.cloned.1.call-done), kind=kLoop, calls=%fused_computation.207 | loop fusion | bytes 50331648 | tf_op jit(solution)/shard_map/slice | solution.py:103
  269.4 50.6 %copy.668 = bf16[1,1024,6144]{1,2,0:T(8,128)(2,1)} copy(bf16[1,1024,6144]{2,0,1:T(2,128)(2,1)} %get-tuple-element.27) | data formatting | bytes 25165824
  320.0 7.0 %convolution_bitcast_fusion.1 = f32[3072,256]{0,1:T(8,128)S(1)} fusion(bf16[1024,2,3072]{0,2,1:T(8,128)(2,1)} %bitcast.405, bf16[1,1024,256]{1,2,0:T(8,128)(2,1)S(1)} %copy-done.6, bf16[1,1024,256]{1,2,0:T(8,128)(2,1)S(1)} %get-tuple-element.258), kind=kOutput, calls=%fused_computation.5 | convolution fusion | flops 3221749760 | bytes 16777216 | tf_op jit(solution)/shard_map/dot_general | solution.py:40
  327.0 1.4 fusion.39
  328.5 1.9 copy.528
  330.4 2.0 fusion.47
  332.9 1.4 fusion.46
  337.1 6.0 multiply_add_fusion.1
  343.1 5.9 multiply_subtract_fusion.1
  349.0 50.6 %copy.669 = bf16[1,1024,6144]{1,2,0:T(8,128)(2,1)} copy(bf16[1,1024,6144]{2,0,1:T(2,128)(2,1)} %get-tuple-element.26) | data formatting | bytes 25165824
  399.7 6.6 %convolution_bitcast_fusion = f32[3072,256]{0,1:T(8,128)S(1)} fusion(bf16[1024,2,3072]{0,2,1:T(8,128)(2,1)} %bitcast.404, bf16[1,1024,256]{1,2,0:T(8,128)(2,1)S(1)} %copy-done.7, bf16[1,1024,256]{1,2,0:T(8,128)(2,1)S(1)} %copy-done.5), kind=kOutput, calls=%fused_computation.4 | convolution fusion | flops 3221749760 | bytes 16777216 | tf_op jit(solution)/shard_map/dot_general | solution.py:40
  406.3 1.4 fusion.38
  407.7 1.9 copy.599
  409.6 2.0 fusion.45
  412.2 1.4 fusion.44
  416.3 5.3 multiply_add_fusion
  421.6 5.5 multiply_subtract_fusion
  427.3 1.3 copy-done.1
  430.2 10.9 %fusion.23 = (f32[16,128]{1,0:T(8,128)S(1)}, f32[16,128]{1,0:T(8,128)S(1)}) fusion(f32[12,16,128]{2,1,0:T(8,128)S(1)} %copy-done.43, f32[12]{0:T(128)} %get-tuple-element.280, f32[16,16,128]{2,1,0:T(8,128)S(1)} %copy-done.9, f32[12,16,128]{2,1,0:T(8,128)S(1)} %copy-done.42, f32[16,128]{1,0:T(8,128)} %get-tuple-element.263, ...), kind=kLoop, calls=%fused_computation.45 | loop fusion | flops 58585088 | bytes 3760176 | tf_op jit(solution)/shard_map/reduce_sum | solution.py:87
  441.3 10.3 %fusion.21 = (f32[16,128]{1,0:T(8,128)S(1)}, f32[16,128]{1,0:T(8,128)S(1)}) fusion(f32[12,16,128]{2,1,0:T(8,128)S(1)} %copy-done.41, f32[12]{0:T(128)} %get-tuple-element.279, f32[16,16,128]{2,1,0:T(8,128)S(1)} %copy-done.8, f32[12,16,128]{2,1,0:T(8,128)S(1)} %copy-done.40, f32[16,128]{1,0:T(8,128)} %get-tuple-element.261, ...), kind=kLoop, calls=%fused_computation.43 | loop fusion | flops 58585088 | bytes 3760176 | tf_op jit(solution)/shard_map/reduce_sum | solution.py:87
  451.6 1.0 fusion.29
  454.0 91.7 %all-reduce = f32[512]{0:T(512)S(1)} all-reduce(f32[512]{0:T(512)S(1)} %convert_reduce_fusion), channel_id=3, replica_groups=mesh['grp'=4,'kp'=32] {'kp'}, use_global_device_ids=true, to_apply=%region_6.9.clone | all-reduce | flops 512 | bytes 4096
  545.8 88.3 %reduce-scatter.2.cloned.1.call-done = f32[16,32]{1,0:T(8,128)} async-done(((f32[512,32]{1,0:T(8,128)}), f32[16,32]{1,0:T(8,128)}) %reduce-scatter.2.cloned.1.call-update) | async-done | bytes 2064 | tf_op jit(solution)/shard_map/reduce_scatter | solution.py:124
  (465 shorter events, 44.3 us)
Async XLA Ops:
  7.2 3.1 copy-start.141
  7.2 3.1 copy-start.139
  7.2 5.3 copy-start.3
  7.2 7.4 %copy-start.155 = (s32[2,128]{1,0:T(2,128)S(1)}, s32[2,128]{1,0:T(2,128)}, u32[]{:S(2)}) copy-start(s32[2,128]{1,0:T(2,128)} %param.20) | copy-start | bytes 3076
  7.2 7.5 %copy-start.140 = (s32[3,1024]{1,0:T(4,128)S(1)}, s32[3,1024]{1,0:T(4,128)}, u32[]{:S(2)}) copy-start(s32[3,1024]{1,0:T(4,128)} %param.14) | copy-start | bytes 36868
  7.2 215.1 %all-gather.2.cloned.1.call-start = ((), (), s32[]{:S(2)}) async-start(), calls=%async_computation.1 | async-start | bytes 25952256 | tf_op jit(solution)/shard_map/all_gather | solution.py:99
  10.2 10.3 %copy-start.152 = (f32[2,12]{1,0:T(2,128)S(1)}, f32[2,12]{1,0:T(2,128)}, u32[]{:S(2)}) copy-start(f32[2,12]{1,0:T(2,128)} %param.18) | copy-start | bytes 292
  10.2 11.0 %copy-start.154 = (f32[2,2,12]{2,1,0:T(2,128)S(1)}, f32[2,2,12]{2,1,0:T(2,128)}, u32[]{:S(2)}) copy-start(f32[2,2,12]{2,1,0:T(2,128)} %param.19) | copy-start | bytes 580
  10.2 623.9 %reduce-scatter.2.cloned.1.call-start = ((), (), s32[]{:S(2)}) async-start(), calls=%async_computation.2 | async-start | bytes 270336 | tf_op jit(solution)/shard_map/reduce_scatter | solution.py:124
  10.4 12.8 %collective-permute-start.3 = (f32[2,16,128]{1,0,2:T(2,128)S(1)}, f32[2,16,128]{1,0,2:T(2,128)S(1)}, u32[]{:S(2)}, u32[]{:S(2)}) collective-permute-start(f32[2,16,128]{1,0,2:T(2,128)S(1)} %copy.591), channel_id=1, source_target_pairs={{0,64},{32,96},{64,0},{96,32},{1,65},{33,97},{65,1},{97,33},{2,66}... | collective-permute-start | bytes 49160 | tf_op jit(solution)/shard_map/ppermute | solution.py:19
  12.5 11.5 %collective-permute-start.1 = (f32[2,16,128]{1,0,2:T(2,128)S(1)}, f32[2,16,128]{1,0,2:T(2,128)S(1)}, u32[]{:S(2)}, u32[]{:S(2)}) collective-permute-start(f32[2,16,128]{1,0,2:T(2,128)S(1)} %copy.591), channel_id=1, source_target_pairs={{0,96},{32,0},{64,32},{96,64},{1,97},{33,1},{65,33},{97,65},{2,98}... | collective-permute-start | bytes 49160 | tf_op jit(solution)/shard_map/ppermute | solution.py:19
  12.5 15.9 %collective-permute-start.2 = (f32[2,16,16,128]{3,2,1,0:T(8,128)S(1)}, f32[2,16,16,128]{3,2,1,0:T(8,128)}, u32[]{:S(2)}, u32[]{:S(2)}) collective-permute-start(f32[2,16,16,128]{3,2,1,0:T(8,128)S(1)} %copy-done.3), channel_id=1, source_target_pairs={{0,64},{32,96},{64,0},{96,32},{1,65},{33,97},{65,1},{97,33},{2,66}... | collective-permute-start | bytes 786440 | tf_op jit(solution)/shard_map/ppermute | solution.py:19
  13.7 18.8 %collective-permute-start = (f32[2,16,16,128]{3,2,1,0:T(8,128)S(1)}, f32[2,16,16,128]{3,2,1,0:T(8,128)S(1)}, u32[]{:S(2)}, u32[]{:S(2)}) collective-permute-start(f32[2,16,16,128]{3,2,1,0:T(8,128)S(1)} %copy-done.3), channel_id=1, source_target_pairs={{0,96},{32,0},{64,32},{96,64},{1,97},{33,1},{65,33},{97,65},{2,98}... | collective-permute-start | bytes 786440 | tf_op jit(solution)/shard_map/ppermute | solution.py:19
  14.7 10.1 %copy-start.144 = (pred[128]{0:T(512)(128)(4,1)}, pred[128]{0:T(512)(128)(4,1)S(1)}, u32[]{:S(2)}) copy-start(pred[128]{0:T(512)(128)(4,1)S(1)} %get-tuple-element.20) | copy-start | bytes 388
  14.7 10.1 %copy-start.146 = (pred[128]{0:T(512)(128)(4,1)}, pred[128]{0:T(512)(128)(4,1)S(1)}, u32[]{:S(2)}) copy-start(pred[128]{0:T(512)(128)(4,1)S(1)} %get-tuple-element.283) | copy-start | bytes 388
  14.7 8.5 %copy-start.142 = (s32[1024]{0:T(1024)}, s32[1024]{0:T(1024)S(1)}, u32[]{:S(2)}) copy-start(s32[1024]{0:T(1024)S(1)} %pad_clamp_fusion) | copy-start | bytes 12292
  20.5 299.5 %copy-start.4 = (bf16[1,1024,256]{1,2,0:T(8,128)(2,1)}, bf16[1,1024,256]{1,2,0:T(8,128)(2,1)S(1)}, u32[]{:S(2)}) copy-start(bf16[1,1024,256]{1,2,0:T(8,128)(2,1)S(1)} %get-tuple-element.258) | copy-start | bytes 1572868
  23.1 5.2 copy-start.143
  32.4 3.0 copy-start.145
  32.4 3.0 copy-start.147
  38.1 1.4 copy-start
  269.4 50.6 %copy-start.6 = (bf16[1,1024,256]{1,2,0:T(8,128)(2,1)S(1)}, bf16[1,1024,256]{1,2,0:T(8,128)(2,1)}, u32[]{:S(2)}) copy-start(bf16[1,1024,256]{1,2,0:T(8,128)(2,1)} %get-tuple-element.259) | copy-start | bytes 1572868
  332.9 1.5 copy-start.38
  332.9 1.6 copy-start.36
  332.9 1.7 copy-start.34
  334.4 1.1 copy-start.28
  334.4 1.2 copy-start.26
  334.5 1.2 copy-start.24
  334.6 1.2 copy-start.22
  334.7 1.5 copy-start.20
  335.3 1.0 copy-start.18
  349.0 50.7 %copy-start.5 = (bf16[1,1024,256]{1,2,0:T(8,128)(2,1)S(1)}, bf16[1,1024,256]{1,2,0:T(8,128)(2,1)}, u32[]{:S(2)}) copy-start(bf16[1,1024,256]{1,2,0:T(8,128)(2,1)} %copy-done.4) | copy-start | bytes 1572868
  349.0 50.7 %copy-start.7 = (bf16[1,1024,256]{1,2,0:T(8,128)(2,1)S(1)}, bf16[1,1024,256]{1,2,0:T(8,128)(2,1)}, u32[]{:S(2)}) copy-start(bf16[1,1024,256]{1,2,0:T(8,128)(2,1)} %get-tuple-element.259) | copy-start | bytes 1572868
  412.2 1.5 copy-start.39
  412.2 1.6 copy-start.37
  412.2 1.7 copy-start.35
  413.6 1.1 copy-start.29
  413.7 1.2 copy-start.27
  413.8 1.2 copy-start.25
  413.9 1.2 copy-start.23
  414.0 1.5 copy-start.21
  414.6 1.0 copy-start.19
  421.6 5.5 copy-start.2
  427.1 1.4 copy-start.1
  428.8 1.0 copy-start.43
  428.8 1.0 copy-start.105
  430.0 11.1 %copy-start.8 = (f32[16,16,128]{2,1,0:T(8,128)S(1)}, f32[16,16,128]{2,1,0:T(8,128)}, u32[]{:S(2)}) copy-start(f32[16,16,128]{2,1,0:T(8,128)} %get-tuple-element.271) | copy-start | bytes 393220
  430.0 11.1 %copy-start.40 = (f32[12,16,128]{2,1,0:T(8,128)S(1)}, f32[12,16,128]{2,1,0:T(8,128)}, u32[]{:S(2)}) copy-start(f32[12,16,128]{2,1,0:T(8,128)} %get-tuple-element.269) | copy-start | bytes 294916
  430.0 11.1 %copy-start.41 = (f32[12,16,128]{2,1,0:T(8,128)S(1)}, f32[12,16,128]{2,1,0:T(8,128)}, u32[]{:S(2)}) copy-start(f32[12,16,128]{2,1,0:T(8,128)} %get-tuple-element.270) | copy-start | bytes 294916
  430.0 11.1 %copy-start.123 = (f32[16,128]{1,0:T(8,128)S(1)}, f32[16,128]{1,0:T(8,128)}, u32[]{:S(2)}) copy-start(f32[16,128]{1,0:T(8,128)} %copy.661) | copy-start | bytes 24580
  430.1 11.1 %copy-start.124 = (f32[16,128]{1,0:T(8,128)S(1)}, f32[16,128]{1,0:T(8,128)}, u32[]{:S(2)}) copy-start(f32[16,128]{1,0:T(8,128)} %copy.660) | copy-start | bytes 24580
  430.1 11.1 %copy-start.125 = (f32[16,128]{1,0:T(8,128)S(1)}, f32[16,128]{1,0:T(8,128)}, u32[]{:S(2)}) copy-start(f32[16,128]{1,0:T(8,128)} %copy.659) | copy-start | bytes 24580
  430.1 11.1 %copy-start.126 = (f32[16,128]{1,0:T(8,128)S(1)}, f32[16,128]{1,0:T(8,128)}, u32[]{:S(2)}) copy-start(f32[16,128]{1,0:T(8,128)} %copy.658) | copy-start | bytes 24580
  430.1 11.1 %copy-start.127 = (f32[16,128]{1,0:T(8,128)S(1)}, f32[16,128]{1,0:T(8,128)}, u32[]{:S(2)}) copy-start(f32[16,128]{1,0:T(8,128)} %copy.657) | copy-start | bytes 24580
  430.1 11.1 %copy-start.128 = (f32[16,128]{1,0:T(8,128)S(1)}, f32[16,128]{1,0:T(8,128)}, u32[]{:S(2)}) copy-start(f32[16,128]{1,0:T(8,128)} %copy.656) | copy-start | bytes 24580
  430.1 11.1 %copy-start.129 = (f32[16,128]{1,0:T(8,128)S(1)}, f32[16,128]{1,0:T(8,128)}, u32[]{:S(2)}) copy-start(f32[16,128]{1,0:T(8,128)} %copy.655) | copy-start | bytes 24580
  430.1 11.1 %copy-start.130 = (f32[16,128]{1,0:T(8,128)S(1)}, f32[16,128]{1,0:T(8,128)}, u32[]{:S(2)}) copy-start(f32[16,128]{1,0:T(8,128)} %copy.654) | copy-start | bytes 24580
  430.1 11.1 %copy-start.131 = (f32[16,128]{1,0:T(8,128)S(1)}, f32[16,128]{1,0:T(8,128)}, u32[]{:S(2)}) copy-start(f32[16,128]{1,0:T(8,128)} %copy.653) | copy-start | bytes 24580
  430.1 11.1 %copy-start.133 = (f32[16,128]{1,0:T(8,128)S(1)}, f32[16,128]{1,0:T(8,128)}, u32[]{:S(2)}) copy-start(f32[16,128]{1,0:T(8,128)} %copy.652) | copy-start | bytes 24580
  430.1 11.1 %copy-start.135 = (f32[16,128]{1,0:T(8,128)S(1)}, f32[16,128]{1,0:T(8,128)}, u32[]{:S(2)}) copy-start(f32[16,128]{1,0:T(8,128)} %copy.651) | copy-start | bytes 24580
  430.2 11.1 %copy-start.137 = (f32[16,128]{1,0:T(8,128)S(1)}, f32[16,128]{1,0:T(8,128)}, u32[]{:S(2)}) copy-start(f32[16,128]{1,0:T(8,128)} %copy.650) | copy-start | bytes 24580
  441.3 10.4 %copy-start.153 = (s32[128]{0:T(128)S(1)}, s32[128]{0:T(128)}, u32[]{:S(2)}) copy-start(s32[128]{0:T(128)} %param.21) | copy-start | bytes 1540
  441.3 11.5 %copy-start.156 = (u32[128]{0:T(128)S(1)}, u32[128]{0:T(128)}, u32[]{:S(2)}) copy-start(u32[128]{0:T(128)} %constant.98) | copy-start | bytes 1540
  451.6 183.9 %copy-start.104 = (f32[2,16,128]{2,1,0:T(8,128)}, f32[2,16,128]{2,1,0:T(8,128)S(1)}, u32[]{:S(2)}) copy-start(f32[2,16,128]{2,1,0:T(8,128)S(1)} %fusion.31) | copy-start | bytes 49156
  (99 other events, 93.3 us)
Sparse Core Ops, SparseCore 0:
  11.0 211.2 all-gather.1
  452.7 181.3 reduce-scatter.1
where the time goes:
time: 649 us; the launch traced here: 643 us
  local copies, waits for them, and re-layouts  262 us (40%)
  waiting for transfers between devices  196 us (30%)
  blocking collectives  91.7 us (14%)
  other arithmetic  55.6 us (9%)
  between operations  18 us (3%)
  matrix products  14.6 us (2%)
    unnamed x319, local copies, waits for them, and re-layouts  110 us
    all_gather x1, waiting for transfers between devices, local(): gathered = lax.all_gather(g_real, 'kp', axis=1, tiled=True)  108 us
    unnamed x1, blocking collectives  91.7 us
    reduce_scatter x1, waiting for transfers between devices, local(): lax.psum_scatter(partial_sums, 'kp', scatter_dimension=0, tiled=True)  88.3 us
    mul x68, local copies, waits for them, and re-layouts, contribution(): bloch_re = bloch_re + rot_re * part_re + rot_im * part_im  64.8 us
    slice x1, local copies, waits for them, and re-layouts, local(): vertex = fourier(gathered[step], phases)  47.1 us
    reduce_sum x2, other arithmetic, contribution(): return jnp.stack([real_part.sum((0, 1)), imag_part.sum((0, 1))])  21.2 us
    dot_general x2, matrix products, fourier(): lax.dot_general(split, phases, (((0, 1), (1, 0)), ((), ())), preferred_el...  13.6 us
  transfers between devices with their start and end apart: 6, of which 2 were waited for; matrix products, arithmetic and copies ran while one was open for 15% of the time, Pallas kernels for 0%

commit v1 on v0

v1 whole, which is shorter than its diff:
```python
import math
import jax
import jax.numpy as jnp
from jax import lax
from jax.experimental import pallas as pl
from jax.experimental.pallas import tpu as pltpu
from jax.sharding import PartitionSpec as P

KT = 0.025
ETA = 0.05
NKM = 40
F32, BF16 = jnp.float32, jnp.bfloat16
NT = (((1,), (1,)), ((), ()))


def mod_mesh(values):
    return values - NKM * jnp.floor((values + 0.5) * (1.0 / NKM))


def turn(steps):
    x = (steps - 20.0) * (1.0 / 20.0)
    y = x * x
    pi2 = math.pi * math.pi
    cos, sin = 0.0, 0.0
    for n in range(8, -1, -1):
        cos = cos * y + (-1.0) ** n * math.pi ** (2 * n) / math.factorial(2 * n)
        sin = sin * y + (-1.0) ** n * math.pi ** (2 * n + 1) / math.factorial(2 * n + 1)
    return -cos, -(sin * x)


def swap_bits(parts, width, masks):
    parts = list(parts)
    span = len(parts)
    bit = 1
    while bit < span:
        mask = masks[bit * width]
        for low in range(span):
            if low & bit:
                continue
            a, b = parts[low], parts[low | bit]
            parts[low] = jnp.where(mask, pltpu.roll(b, bit * width, 1), a)
            parts[low | bit] = jnp.where(mask, b, pltpu.roll(a, 128 - bit * width, 1))
        bit *= 2
    return parts


def pieces(x, count):
    out = []
    for _ in range(count):
        head = x.astype(BF16)
        out.append(head)
        x = x - head.astype(F32)
    return out


def dot(a, b):
    return jnp.dot(a, b, preferred_element_type=F32)


def dot_nt(a, b):
    return lax.dot_general(a, b, NT, preferred_element_type=F32)


def compute_kernel(where, g_ref, u_ref, e_ref, lat_ref, kq_ref, freq_ref, froh_ref, out_ref,
                   ac, as_, bc, bs, ph, vs, yk, xs, t1, t2, ex, fa, sums, rep, diag, perm):
    zh0, g0, bases = where(froh_ref)
    step = zh0
    mode0 = g0 * 3
    lane = lax.broadcasted_iota(jnp.int32, (8, 128), 1)
    masks = {s: (lane & s) != 0 for s in (1, 2, 4, 8, 16, 32, 64)}

    lat = lat_ref[...].astype(F32)
    n1 = lax.broadcasted_iota(jnp.int32, (40, 1024), 0).astype(F32)
    ac[...], as_[...] = turn(mod_mesh(n1 * lat[0:1]))
    row16 = lax.broadcasted_iota(jnp.int32, (16, 1024), 0).astype(F32)
    for s in range(8):
        i0 = row16 * 8.0 + bases[s].astype(F32)
        q2 = jnp.floor((i0 + 0.5) * (1.0 / 40.0))
        n2 = mod_mesh(q2)
        n3 = mod_mesh(jnp.floor((i0 + 0.5) * (1.0 / 1600.0)))
        bc[16 * s:16 * s + 16], bs[16 * s:16 * s + 16] = turn(mod_mesh(n2 * lat[1:2] + n3 * lat[2:3]))
    rr = lax.broadcasted_iota(jnp.int32, (128, 2048), 0)
    rl = lax.broadcasted_iota(jnp.int32, (128, 2048), 1)
    rep[...] = jnp.where(rl // 16 == rr, 1.0, 0.0).astype(BF16)
    sr = lax.broadcasted_iota(jnp.int32, (128, 128), 0)
    sl = lax.broadcasted_iota(jnp.int32, (128, 128), 1)
    diag[...] = jnp.where(sr // 16 == sl // 16, 1.0, 0.0).astype(BF16)
    eye = jnp.where(sr == sl, 1.0, 0.0).astype(BF16)
    order = kq_ref[pl.ds(step, 1), :]
    onehot = jnp.where(sr == order, 1.0, 0.0)
    perm[...] = onehot.T.astype(BF16)
    lanes768 = lax.broadcasted_iota(jnp.int32, (1, 256), 1)
    onsite = jnp.where(lanes768 // 16 == lanes768 % 16, 1.0, 0.0)
    fro = [jnp.concatenate([onsite * froh_ref[step, c, mode0 + m] for m in range(3)], 1) for c in range(2)]

    for s in range(8):
        own = pieces(e_ref[s, 0:16], 3)
        far = (s // 4) * 4 + lax.rem(s % 4 + step + 1, 4)
        far_e = pieces(e_ref[far, 0:16], 3) + [e_ref[far, 16:32].astype(BF16)]
        moved = dot_nt(jnp.concatenate(far_e, 0), perm[...]).astype(BF16)
        both = dot(jnp.concatenate(own + [moved], 0), rep[...])
        ex[s * 16:s * 16 + 16] = both[0:16] + both[16:32] + both[32:48]
        fe = both[48:64] + both[64:80] + both[80:96]
        fm = both[96:112]
        r16 = lax.broadcasted_iota(jnp.int32, (16, 2048), 0)
        l16 = lax.broadcasted_iota(jnp.int32, (16, 2048), 1) % 16
        pick = r16 == l16
        fe = jnp.where(pick, fe, 0.0).sum(0, keepdims=True)
        fm = jnp.where(pick, fm, 0.0).sum(0, keepdims=True)
        fa[s * 8:s * 8 + 1] = fe
        fa[s * 8 + 1:s * 8 + 2] = fm
        fa[s * 8 + 2:s * 8 + 3] = 1.0 / (jnp.exp(fe * (1.0 / KT)) + 1.0)

    bose, phonon = [], []
    for m in range(3):
        w = jnp.full((1, 128), freq_ref[step, mode0 + m], F32)
        phonon.append(w)
        bose.append(1.0 / (jnp.exp(w / KT) - 1.0))

    def blocks(src, c):
        for hi in range(2):
            for half in range(2):
                col = c * 2 + hi
                parts = [src[col, pl.ds(half * 64 + k, 8, stride=8), :] for k in range(8)]
                parts = swap_bits(parts, 16, masks)
                yield hi, half, parts

    def one_set(s, carry):
        base = bases_at(s)
        def pair(o2, carry2):
            cs, sn = [], []
            for h in range(2):
                o = o2 * 2 + h
                start = pl.multiple_of(lax.rem(base + o * 8, NKM), 8)
                a_c, a_s = ac[pl.ds(start, 8)], as_[pl.ds(start, 8)]
                b_c, b_s = bc[pl.ds(s * 16 + o, 1)], bs[pl.ds(s * 16 + o, 1)]
                cs.append(a_c * b_c - a_s * b_s)
                sn.append(a_s * b_c + a_c * b_s)
            co = jnp.concatenate(cs, 0).astype(BF16)
            si = jnp.concatenate(sn, 0).astype(BF16)
            at = pl.multiple_of(o2 * 16, 16)
            ph[pl.ds(at, 16), 0:1024] = co
            ph[pl.ds(at, 16), 1024:2048] = -si
            at = pl.multiple_of(o2 * 16 + 128, 16)
            ph[pl.ds(at, 16), 0:1024] = si
            ph[pl.ds(at, 16), 1024:2048] = co
            return carry2
        lax.fori_loop(0, 8, pair, 0)
        for c in range(2):
            ver = dot(ph[c * 128:c * 128 + 128], g_ref[...]) + fro[c]
            for tile in range(6):
                vs[c * 6 + tile] = ver[:, tile * 128:tile * 128 + 128]
        far = (s // 4) * 4 + lax.rem(lax.rem(s, 4) + step + 1, 4)
        for w, left, at in ((0, eye, s), (1, perm[...], far)):
            turned = dot_nt(left, u_ref[at])
            for tile in range(4):
                yk[tile] = turned[:, tile * 128:tile * 128 + 128]
            for c in range(2):
                for hi, half, parts in blocks(yk, c):
                    for b in range(8):
                        xs[w * 2 + c, pl.ds(half * 128 + hi * 8 + b, 8, stride=16), :] = parts[b]
        for c in range(2):
            for m in range(3):
                for hi in range(2):
                    for half in range(2):
                        col = c * 6 + m * 2 + hi
                        parts = [vs[col, pl.ds(half * 64 + k, 8, stride=8), :] for k in range(8)]
                        parts = swap_bits(parts, 16, masks)
                        for a in range(8):
                            t1[c, pl.ds(half * 384 + m * 16 + hi * 8 + a, 8, stride=48), :] = parts[a]

        def rows_of(ref, o):
            rows = slice(o * 48, o * 48 + 48)
            return jnp.concatenate([ref[0, rows], ref[1, rows]], 1).astype(BF16)

        def block_matrix(w, o, sign):
            xr = xs[w * 2, o * 16:o * 16 + 16].astype(BF16)
            xi = xs[w * 2 + 1, o * 16:o * 16 + 16].astype(BF16)
            d = diag[...]
            wr = jnp.concatenate([xr] * 8, 0) * d
            wi = jnp.concatenate([xi] * 8, 0) * d
            wn = jnp.concatenate([-xi] * 8, 0) * d
            if sign > 0:
                return jnp.concatenate([jnp.concatenate([wr, wi], 1), jnp.concatenate([wn, wr], 1)], 0)
            return jnp.concatenate([jnp.concatenate([wr, wn], 1), jnp.concatenate([wi, wr], 1)], 0)

        for o in range(16):
            mixed = dot(rows_of(t1, o), block_matrix(0, o, 1))
            t2[0, o * 48:o * 48 + 48] = mixed[:, 0:128]
            t2[1, o * 48:o * 48 + 48] = mixed[:, 128:256]
        for c in range(2):
            for m in range(3):
                for half in range(2):
                    at = half * 384 + m * 16
                    parts = [t2[c, pl.ds(at + a, 8, stride=48), :] for a in range(16)]
                    parts = swap_bits(parts, 1, masks)
                    for n in range(16):
                        t1[c, pl.ds(at + n, 8, stride=48), :] = parts[n]
        for o in range(16):
            bl = dot(rows_of(t1, o), block_matrix(1, o, -1))
            br, bi = bl[:, 0:128], bl[:, 128:256]
            strength = br * br + bi * bi
            cols = slice(o * 128, o * 128 + 128)
            eo = ex[pl.ds(pl.multiple_of(s * 16, 16), 16), cols]
            rows = fa[pl.ds(pl.multiple_of(s * 8, 8), 8), cols]
            fe, fm, occ = rows[0:1], rows[1:2], rows[2:3]
            diff = eo - fe
            re, im = 0.0, 0.0
            for m in range(3):
                em = fm * (bose[m] + occ)
                ab = fm * (bose[m] + 1.0 - occ)
                up = diff + phonon[m]
                lo = diff - phonon[m]
                du = up * up + ETA * ETA
                dl = lo * lo + ETA * ETA
                scale = strength[m * 16:m * 16 + 16] / (du * dl)
                e1 = em * dl
                a1 = ab * du
                re = re + scale * (e1 * up + a1 * lo)
                im = im + scale * (e1 + a1)
            sums[pl.ds(pl.multiple_of(s * 32, 32), 16), cols] = re
            sums[pl.ds(pl.multiple_of(s * 32 + 16, 16), 16), cols] = im * (-ETA)
        return carry

    def bases_at(s):
        return bases[0] + lax.rem(s, 4) * 4096 + (s // 4) * 512

    lax.fori_loop(0, 8, one_set, 0)
    hi, lo = pieces(sums[...], 2)
    out_ref[...] = (dot_nt(hi, rep[...]) + dot_nt(lo, rep[...])) * (1.0 / 384.0)


def compute(where, g, u, e, lat, kq, freq, froh):
    vm = pl.BlockSpec(memory_space=pltpu.VMEM)
    sm = pl.BlockSpec(memory_space=pltpu.SMEM)
    return pl.pallas_call(
        lambda *refs: compute_kernel(where, *refs),
        out_shape=jax.ShapeDtypeStruct((256, 128), F32),
        in_specs=[vm, vm, vm, vm, vm, sm, sm],
        out_specs=vm,
        scratch_shapes=[
            pltpu.VMEM((40, 1024), F32), pltpu.VMEM((40, 1024), F32),
            pltpu.VMEM((128, 1024), F32), pltpu.VMEM((128, 1024), F32),
            pltpu.VMEM((256, 2048), BF16),
            pltpu.VMEM((12, 128, 128), F32),
            pltpu.VMEM((4, 128, 128), F32),
            pltpu.VMEM((4, 256, 128), F32),
            pltpu.VMEM((2, 768, 128), F32), pltpu.VMEM((2, 768, 128), F32),
            pltpu.VMEM((128, 2048), F32), pltpu.VMEM((64, 2048), F32),
            pltpu.VMEM((256, 2048), F32),
            pltpu.VMEM((128, 2048), BF16), pltpu.VMEM((128, 128), BF16), pltpu.VMEM((128, 128), BF16),
        ],
        compiler_params=pltpu.CompilerParams(vmem_limit_bytes=50 * 2 ** 20),
    )(g, u, e, lat, kq, freq, froh)


MESH = pl.DeviceIdType.MESH


def position():
    kp = lax.axis_index("kp")
    return lax.axis_index("grp"), kp // 8, kp // 4 % 2, kp % 4


def at(g, x, zh, y):
    return (g, x * 8 + zh * 4 + y)


def column(g, zh):
    for hop in range(1, 8):
        other = (zh * 4 + g + hop) % 8
        yield hop, other % 4, other // 4


def greet(devices):
    barrier = pltpu.get_barrier_semaphore()
    for device in devices:
        pl.semaphore_signal(barrier, inc=1, device_id=device, device_id_type=MESH)
    pl.semaphore_wait(barrier, len(devices))


def gather_kernel(g_ref, u_ref, en_ref, mask_ref, gbuf, ubuf, ebuf,
                  local_sem, z_send, z_recv, u_send, u_recv, e_send, e_recv, g_send, g_recv):
    g, x, zh, y = position()
    mine = zh * 4 + g
    others = [at(g2, x, zh2, y) for _, g2, zh2 in column(g, zh)]
    for hop in range(1, 4):
        others.append(at(g, (x + hop) % 4, zh, y))
        others.append(at(g, x, zh, (y + hop) % 4))
    greet(others)

    def remote(src, dst, send, recv, device):
        return pltpu.make_async_remote_copy(src_ref=src, dst_ref=dst, send_sem=send, recv_sem=recv,
                                            device_id=device, device_id_type=MESH)

    def part(step, triple, c):
        return g_ref.at[step, :, pl.ds(pl.multiple_of(c * 3072 + triple * 768, 768), 768)]

    pz, pg = 1 - zh, (g + 2) % 4
    first = []
    for c in range(2):
        far = remote(part(pz, pg, c), gbuf.at[c, x, zh, y], z_send.at[c], z_recv.at[c], at(pg, x, pz, y))
        far.start()
        near = pltpu.make_async_copy(part(zh, g, c), gbuf.at[c, x, zh, y], local_sem.at[c])
        near.start()
        first.append((far, near))
    ubuf[mine] = u_ref[...].astype(BF16)
    ebuf[mine, 0:16] = en_ref[...]
    ebuf[mine, 16:32] = mask_ref[...].astype(F32)
    small = []
    for hop, g2, zh2 in column(g, zh):
        small.append(remote(ubuf.at[mine], ubuf.at[mine], u_send.at[hop], u_recv.at[hop], at(g2, x, zh2, y)))
        small.append(remote(ebuf.at[mine], ebuf.at[mine], e_send.at[hop], e_recv.at[hop], at(g2, x, zh2, y)))
    sent = []

    def to_x(c, ys, hop, sem):
        piece = gbuf.at[c, x, :, ys]
        copy = remote(piece, piece, g_send.at[c, sem], g_recv.at[c, sem], at(g, (x + hop) % 4, zh, y))
        copy.start()
        sent.append(copy)

    def to_y(c, xs, hop, sem):
        piece = gbuf.at[c, xs, :, y]
        copy = remote(piece, piece, g_send.at[c, sem], g_recv.at[c, sem], at(g, x, zh, (y + hop) % 4))
        copy.start()
        sent.append(copy)

    for far, near in first:
        near.wait()
        far.wait()
    for hop in (1, 3, 2):
        to_x(0, y, hop, 16 + hop)
        to_y(1, x, hop, 16 + hop)
    for copy in small:
        copy.start()
    for hop in (1, 3, 2):
        to_y(0, x, hop, hop)
        to_x(1, y, hop, hop)
    for hop in (1, 3, 2):
        xs, ys = (x + 4 - hop) % 4, (y + 4 - hop) % 4
        got = gbuf.at[0, xs, :, y]
        remote(got, got, g_send.at[0, 16 + hop], g_recv.at[0, 16 + hop], at(g, xs, zh, y)).wait_recv()
        for to in (1, 3, 2):
            to_y(0, xs, to, 4 * hop + to)
        got = gbuf.at[1, x, :, ys]
        remote(got, got, g_send.at[1, 16 + hop], g_recv.at[1, 16 + hop], at(g, x, zh, ys)).wait_recv()
        for to in (1, 3, 2):
            to_x(1, ys, to, 4 * hop + to)
    for copy in small:
        copy.wait()
    for hop in (0, 1, 3, 2):
        for to in (1, 3, 2):
            xs, ys = (x + 4 - hop) % 4, (y + 4 - to) % 4
            got = gbuf.at[0, xs, :, ys]
            remote(got, got, g_send.at[0, 0], g_recv.at[0, 4 * hop + to], at(g, x, zh, ys)).wait_recv()
            xs, ys = (x + 4 - to) % 4, (y + 4 - hop) % 4
            got = gbuf.at[1, xs, :, ys]
            remote(got, got, g_send.at[1, 0], g_recv.at[1, 4 * hop + to], at(g, xs, zh, y)).wait_recv()
    for copy in sent:
        copy.wait_send()


def gather(g_real, u, energy, mask):
    vm = pl.BlockSpec(memory_space=pltpu.VMEM)
    anywhere = pl.BlockSpec(memory_space=pl.ANY)
    dma = pltpu.SemaphoreType.DMA
    return pl.pallas_call(
        gather_kernel,
        out_shape=(jax.ShapeDtypeStruct((2, 4, 2, 4, 32, 768), BF16),
                   jax.ShapeDtypeStruct((8, 512, 128), BF16),
                   jax.ShapeDtypeStruct((8, 32, 128), F32)),
        in_specs=[anywhere, vm, vm, vm],
        out_specs=(vm, vm, vm),
        scratch_shapes=[dma((2,)), dma((2,)), dma((2,)), dma((8,)), dma((8,)), dma((8,)), dma((8,)),
                        dma((2, 20)), dma((2, 20))],
        compiler_params=pltpu.CompilerParams(collective_id=0, has_side_effects=True,
                                             vmem_limit_bytes=40 * 2 ** 20),
    )(g_real, u, energy, mask)


def reduce_kernel(part_ref, irr_ref, sigma_ref, star_ref, got, stars, blocks,
                  a_send, a_recv, b_send, b_recv):
    g, x, zh, y = position()
    me = x * 8 + zh * 4 + y
    mine = zh * 4 + g
    others = [at(g2, x, zh2, y) for _, g2, zh2 in column(g, zh)]
    greet(others + [(g, (me + hop) % 32) for hop in range(1, 32)])
    copies = []
    for hop, g2, zh2 in column(g, zh):
        owner = zh2 * 4 + g2
        copies.append(pltpu.make_async_remote_copy(
            src_ref=part_ref.at[owner], dst_ref=got.at[hop], send_sem=a_send.at[hop],
            recv_sem=a_recv.at[hop], device_id=at(g2, x, zh2, y), device_id_type=MESH))
        copies[-1].start()
    labels = lax.broadcasted_iota(jnp.int32, (512, 128), 0)
    member = jnp.where(labels == irr_ref[...], 1.0, 0.0).astype(BF16)
    total = part_ref[mine]
    for hop, copy in enumerate(copies, 1):
        copy.wait_recv()
        total = total + got[hop]
    sigma_ref[...] = total
    columns = jnp.concatenate(pieces(total, 3) + [jnp.ones((32, 128), BF16)], 0)
    stars[...] = dot_nt(member, columns)
    for hop in range(1, 32):
        owner = (me + hop) % 32
        copies.append(pltpu.make_async_remote_copy(
            src_ref=stars.at[pl.ds(pl.multiple_of(owner * 16, 16), 16)], dst_ref=blocks.at[hop],
            send_sem=b_send.at[hop], recv_sem=b_recv.at[hop], device_id=(g, owner), device_id_type=MESH))
        copies[-1].start()
    mean = stars[pl.ds(pl.multiple_of(me * 16, 16), 16)]
    for hop in range(1, 32):
        copies[6 + hop].wait_recv()
        mean = mean + blocks[hop]
    count = pltpu.roll(mean, 32, 1)
    mean = mean + pltpu.roll(mean, 96, 1) + pltpu.roll(mean, 64, 1)
    star_ref[...] = mean / jnp.maximum(count, 1.0)
    for copy in copies:
        copy.wait_send()


def reduce(part, irr):
    vm = pl.BlockSpec(memory_space=pltpu.VMEM)
    dma = pltpu.SemaphoreType.DMA
    return pl.pallas_call(
        reduce_kernel,
        out_shape=(jax.ShapeDtypeStruct((32, 128), F32), jax.ShapeDtypeStruct((16, 128), F32)),
        in_specs=[vm, vm],
        out_specs=(vm, vm),
        scratch_shapes=[pltpu.VMEM((8, 32, 128), F32), pltpu.VMEM((512, 128), F32),
                        pltpu.VMEM((32, 16, 128), F32),
                        dma((8,)), dma((8,)), dma((32,)), dma((32,))],
        compiler_params=pltpu.CompilerParams(collective_id=1, has_side_effects=True),
    )(part, irr)


def local(g_real, lattice, u_rot, energy, band_mask, freq, froh, kq_index, irr_id):
    def where(_):
        g, x, zh, y = position()
        first = (x * 8 + y) * 128
        return zh, g, [first + s % 4 * 4096 + s // 4 * 512 for s in range(8)]

    vertex, rotations, levels = gather(g_real, u_rot.reshape(512, 128), energy, band_mask)
    part = compute(where, vertex.reshape(2048, 768), rotations, levels, lattice, kq_index, freq, froh)
    sigma, star = reduce(part.reshape(8, 32, 128), irr_id.reshape(1, 128))
    return sigma.reshape(2, 16, 128), star[:, :32].T.reshape(2, 16, 16)


def solution(mesh):
    in_specs = (
        P(None, "kp", None),
        P(),
        P(None, None, None, ("grp", "kp")),
        P(None, ("grp", "kp")),
        P(None, ("grp", "kp")),
        P(),
        P(),
        P(),
        P(("grp", "kp")),
    )
    out_specs = (P(None, None, ("grp", "kp")), P(None, None, ("grp", "kp")))
    return jax.shard_map(local, mesh=mesh, in_specs=in_specs, out_specs=out_specs, check_vma=False)
```

time: 649 us -> 101 us (0.16)
  local copies, waits for them, and re-layouts: 262 us -> 11.2 us
  waiting for transfers between devices: 196 us -> 0 us
  blocking collectives: 91.7 us -> 0 us
  Pallas kernels: 0 us -> 88.5 us
  other arithmetic: 55.6 us -> 0 us
  between operations: 18 us -> 0.69 us
  matrix products: 14.6 us -> 0 us
    all_gather x1 -> x0, waiting for transfers between devices: 108 us -> none  [local(): gathered = lax.all_gather(g_real, 'kp', axis=1, tiled=True)]
    unnamed x319 -> x22, local copies, waits for them, and re-layouts: 110 us -> 10.5 us
    unnamed x1 -> x0, blocking collectives: 91.7 us -> none
    pallas_call x0 -> x3, Pallas kernels: none -> 88.5 us  [the longest x1 35.6 us: compute(): pl.pallas_call(lambda *refs: compute_kernel(where, *refs), out_shape=jax....]
    reduce_scatter x1 -> x0, waiting for transfers between devices: 88.3 us -> none  [local(): lax.psum_scatter(partial_sums, 'kp', scatter_dimension=0, tiled=True)]
    slice x16 -> x0, local copies, waits for them, and re-layouts: 71.9 us -> none  [the longest x1 47.1 us: local(): vertex = fourier(gathered[step], phases)]
    mul x136 -> x0, local copies, waits for them, and re-layouts: 69.1 us -> none  [the longest x68 64.8 us: contribution(): bloch_re = bloch_re + rot_re * part_re + rot_im * part_im]
    reduce_sum x3 -> x0, other arithmetic: 21.4 us -> none  [the longest x2 21.2 us: contribution(): return jnp.stack([real_part.sum((0, 1)), imag_part.sum((0, 1))])]
  transfers between devices with their start and end apart: 6 -> 0, of which waited for: 2 -> 0; matrix products, arithmetic and copies ran while one was open for 15% -> 0% of each run, Pallas kernels for 0% -> 0%
where the time goes in v1:
time: 101 us; the launch traced here: 100 us
  Pallas kernels  88.5 us (88%)
  local copies, waits for them, and re-layouts  11.2 us (11%)
    pallas_call x1, Pallas kernels, compute(): pl.pallas_call(lambda *refs: compute_kernel(where, *refs), out_shape=jax....  35.6 us
    pallas_call x1, Pallas kernels, gather(): pl.pallas_call(gather_kernel, out_shape=(jax.ShapeDtypeStruct((2, 4, 2, 4...  34.9 us
    pallas_call x1, Pallas kernels, reduce(): pl.pallas_call(reduce_kernel, out_shape=(jax.ShapeDtypeStruct((32, 128),...  18.1 us
    unnamed x22, local copies, waits for them, and re-layouts  10.5 us

profile of v1, /device:TPU:0, one launch (start us, length us, event | category | flops | bytes accessed | tf_op | source)
XLA Modules:
  0.0 100.3 jit_solution(8832570382118228628)
XLA Ops:
  0.6 0.0 copy-start.1
  0.6 1.1 %copy-done.1 = bf16[2,32,6144]{2,1,0:T(8,128)(2,1)S(1)} copy-done((bf16[2,32,6144]{2,1,0:T(8,128)(2,1)S(1)}, bf16[2,32,6144]{2,1,0:T(8,128)(2,1)}, u32[]{:S(2)}) %copy-start.1) | copy-done | bytes 786456
  1.8 0.0 copy-start.3
  1.8 0.9 copy-done.3
  2.7 0.0 copy-start.5
  2.7 0.7 copy-done.5
  3.4 0.0 copy-start.6
  3.4 0.7 copy-done.6
  4.1 34.9 %shard_map.104 = (bf16[2,4,2,4,32,768]{5,4,3,2,1,0:T(8,128)(2,1)S(1)}, bf16[8,512,128]{2,1,0:T(8,128)(2,1)S(1)}, f32[8,32,128]{2,1,0:T(8,128)S(1)}) custom-call(bf16[2,32,6144]{2,1,0:T(8,128)(2,1)S(1)} %copy-done.1, f32[512,128]{1,0:T(8,128)S(1)} %bitcast.10, f32[16,128]{1,0:T(8,128)S(1)} %copy-done.5, s32[16,128]{1,0:T(8,128)S(1)} %copy-done.6), custom_call_target="tpu_custom_call" | custom-call | tf_op jit(solution)/shard_map/pallas_call | solution.py:367
  39.0 0.0 copy-start
  39.0 1.6 %copy-done = bf16[2,4,2,4,32,768]{5,4,3,2,1,0:T(8,128)(2,1)} copy-done((bf16[2,4,2,4,32,768]{5,4,3,2,1,0:T(8,128)(2,1)}, bf16[2,4,2,4,32,768]{5,4,3,2,1,0:T(8,128)(2,1)S(1)}, u32[]{:S(2)}) %copy-start) | copy-done | bytes 3145752
  40.6 0.0 copy-start.4
  40.6 0.7 copy-done.4
  41.3 0.0 copy-start.7
  41.3 0.7 copy-done.7
  42.0 0.0 copy-start.8
  42.0 0.7 copy-done.8
  42.7 0.0 copy-start.9
  42.7 0.7 copy-done.9
  43.4 35.6 %shard_map.105 = f32[256,128]{1,0:T(8,128)S(1)} custom-call(bf16[2048,768]{1,0:T(8,128)(2,1)} %bitcast.8, bf16[8,512,128]{2,1,0:T(8,128)(2,1)S(1)} %get-tuple-element.8.refs_1_, f32[8,32,128]{2,1,0:T(8,128)S(1)} %get-tuple-element.9.refs_2_, s32[3,1024]{1,0:T(4,128)S(1)} %copy-done.4, s32[2,128]{1,0:T(2,128)S(1)} %copy-done.8, f32[2,12]{1,0:T(2,128)S(1)} %copy-done.9, ...), custom_call_target="tpu_custom_call" | custom-call | tf_op jit(solution)/shard_map/pallas_call | solution.py:236
  78.9 0.0 copy-start.2
  78.9 0.6 copy-done.2
  79.6 18.1 %shard_map.106 = (f32[32,128]{1,0:T(8,128)}, f32[16,128]{1,0:T(8,128)}) custom-call(f32[8,32,128]{2,1,0:T(8,128)} %bitcast.9, s32[1,128]{1,0:T(1,128)} %bitcast.13), custom_call_target="tpu_custom_call" | custom-call | tf_op jit(solution)/shard_map/pallas_call | solution.py:424
  97.6 0.7 slice_bitcast_fusion
  98.3 0.7 copy.12
  99.0 1.3 %copy.14 = f32[2,16,128]{2,1,0:T(8,128)} copy(f32[2,16,128]{2,1,0:T(8,128)} %bitcast.12) | data formatting | bytes 32768
Async XLA Ops:
  0.6 1.1 %copy-start.1 = (bf16[2,32,6144]{2,1,0:T(8,128)(2,1)S(1)}, bf16[2,32,6144]{2,1,0:T(8,128)(2,1)}, u32[]{:S(2)}) copy-start(bf16[2,32,6144]{2,1,0:T(8,128)(2,1)} %g_ref.1) | copy-start | bytes 2359300
  1.8 0.9 copy-start.3
  2.7 0.7 copy-start.5
  3.4 0.7 copy-start.6
  39.0 1.6 %copy-start = (bf16[2,4,2,4,32,768]{5,4,3,2,1,0:T(8,128)(2,1)}, bf16[2,4,2,4,32,768]{5,4,3,2,1,0:T(8,128)(2,1)S(1)}, u32[]{:S(2)}) copy-start(bf16[2,4,2,4,32,768]{5,4,3,2,1,0:T(8,128)(2,1)S(1)} %get-tuple-element.7) | copy-start | bytes 9437188
  40.6 0.7 copy-start.4
  41.3 0.7 copy-start.7
  42.0 0.7 copy-start.8
  42.7 0.7 copy-start.9
  78.9 0.6 copy-start.2

commit v2 on v0

v2 whole, which is shorter than its diff:
```python
import functools
import math
from types import SimpleNamespace

import jax
import jax.numpy as jnp
from jax import lax
from jax.experimental import pallas as pl
from jax.experimental.pallas import tpu as pltpu
from jax.sharding import PartitionSpec as P

KT = 0.025
ETA = 0.05
NKM = 40
F32, BF16 = jnp.float32, jnp.bfloat16
NT = (((1,), (1,)), ((), ()))
MESH = pl.DeviceIdType.MESH


def mod_mesh(values):
    return values - NKM * jnp.floor((values + 0.5) * (1.0 / NKM))


def turn(steps):
    x = (steps - 20.0) * (1.0 / 20.0)
    y = x * x
    cos, sin = 0.0, 0.0
    for n in range(8, -1, -1):
        cos = cos * y + (-1.0) ** n * math.pi ** (2 * n) / math.factorial(2 * n)
        sin = sin * y + (-1.0) ** n * math.pi ** (2 * n + 1) / math.factorial(2 * n + 1)
    return -cos, -(sin * x)


def pieces(x, count):
    out = []
    for _ in range(count):
        head = x.astype(BF16)
        out.append(head)
        x = x - head.astype(F32)
    return out


def dot(a, b):
    return jnp.dot(a, b, preferred_element_type=F32)


def dot_nt(a, b):
    return lax.dot_general(a, b, NT, preferred_element_type=F32)


def iota(shape, axis):
    return lax.broadcasted_iota(jnp.int32, shape, axis)


def swap_groups(parts):
    parts = list(parts)
    lane = iota(parts[0].shape, 1)
    for bit in (1, 2, 4):
        mask = (lane & (16 * bit)) != 0
        for low in range(8):
            if low & bit == 0:
                a, b = parts[low], parts[low | bit]
                parts[low] = jnp.where(mask, pltpu.roll(b, 16 * bit, 1), a)
                parts[low | bit] = jnp.where(mask, b, pltpu.roll(a, 128 - 16 * bit, 1))
    return parts


def scratch_shapes():
    vm = pltpu.VMEM
    return dict(
        g=vm((3, 2, 4, 2, 4, 32, 256), BF16),
        u=vm((8, 512, 128), BF16),
        e=vm((8, 32, 128), F32),
        ac=vm((40, 1024), F32), as_=vm((40, 1024), F32),
        bc=vm((128, 1024), F32), bs=vm((128, 1024), F32),
        ph=vm((8, 256, 2048), BF16),
        v=vm((2, 1024, 256), BF16),
        xs=vm((2, 8, 3, 256, 128), BF16),
        t1=vm((8, 3, 256, 256), BF16),
        t2=vm((6, 128, 256), BF16),
        t3=vm((6, 256, 128), BF16),
        ex=vm((128, 2048), F32), fa=vm((64, 2048), F32),
        sums=vm((256, 2048), F32),
        rep=vm((128, 2048), BF16), diag=vm((128, 128), BF16), eye=vm((256, 256), BF16),
        mix=vm((256, 256), BF16), perm=vm((128, 128), BF16), turned=vm((128, 128), BF16),
    )


def constants(r):
    rr, rl = iota((128, 2048), 0), iota((128, 2048), 1)
    r.rep[...] = jnp.where(rl // 16 == rr, 1.0, 0.0).astype(BF16)
    sr, sl = iota((128, 128), 0), iota((128, 128), 1)
    r.diag[...] = jnp.where(sr // 16 == sl // 16, 1.0, 0.0).astype(BF16)
    br, bl = iota((256, 256), 0), iota((256, 256), 1)
    r.eye[...] = jnp.where(br == bl, 1.0, 0.0).astype(BF16)
    r.mix[...] = jnp.where((br // 16 == bl % 16) & (br % 16 == bl // 16), 1.0, 0.0).astype(BF16)


def partner_order(r, kq, step):
    sr, sl = iota((128, 128), 0), iota((128, 128), 1)
    order = jnp.where(step == 0, kq[0:1, :], kq[1:2, :])
    perm = jnp.where(sr == order, 1.0, 0.0).T.astype(BF16)
    r.perm[...] = perm
    regroup = jnp.where((sr // 16 == sl % 8) & (sr % 16 == sl // 8), 1.0, 0.0).astype(BF16)
    r.turned[...] = dot(regroup, perm).astype(BF16)


def tables(r, lattice, first):
    lat = lattice.astype(F32)
    r.ac[...], r.as_[...] = turn(mod_mesh(iota((40, 1024), 0).astype(F32) * lat[0:1]))
    row16 = iota((16, 1024), 0).astype(F32)

    def one(s, carry):
        i0 = row16 * 8.0 + first(s).astype(F32) + 0.5
        n2 = mod_mesh(jnp.floor(i0 * (1.0 / 40.0)))
        n3 = mod_mesh(jnp.floor(i0 * (1.0 / 1600.0)))
        rows = pl.ds(pl.multiple_of(s * 16, 16), 16)
        r.bc[rows], r.bs[rows] = turn(mod_mesh(n2 * lat[1:2] + n3 * lat[2:3]))
        return carry

    lax.fori_loop(0, 8, one, 0)


def phases(r, s, first):
    base = first(s)

    def pair(o2, carry):
        cs, sn = [], []
        for h in range(2):
            o = o2 * 2 + h
            rows = pl.ds(pl.multiple_of(lax.rem(base + o * 8, NKM), 8), 8)
            a_c, a_s = r.ac[rows], r.as_[rows]
            b_c, b_s = r.bc[pl.ds(s * 16 + o, 1)], r.bs[pl.ds(s * 16 + o, 1)]
            cs.append(a_c * b_c - a_s * b_s)
            sn.append(a_s * b_c + a_c * b_s)
        co = jnp.concatenate(cs, 0).astype(BF16)
        si = jnp.concatenate(sn, 0)
        up = pl.ds(pl.multiple_of(o2 * 16, 16), 16)
        low = pl.ds(pl.multiple_of(o2 * 16 + 128, 16), 16)
        r.ph[s, up, 0:1024] = co
        r.ph[s, up, 1024:2048] = (-si).astype(BF16)
        r.ph[s, low, 0:1024] = si.astype(BF16)
        r.ph[s, low, 1024:2048] = co
        return carry

    lax.fori_loop(0, 8, pair, 0)


def partner_set(s, step):
    return s // 4 * 4 + lax.rem(lax.rem(s, 4) + step + 1, 4)


def levels(r, s, step):
    own = pieces(r.e[s, 0:16], 3)
    far = partner_set(s, step)
    far_e = pieces(r.e[far, 0:16], 3) + [r.e[far, 16:32].astype(BF16)]
    moved = dot_nt(jnp.concatenate(far_e, 0), r.perm[...]).astype(BF16)
    both = dot(jnp.concatenate(own + [moved], 0), r.rep[...])
    r.ex[pl.ds(pl.multiple_of(s * 16, 16), 16)] = both[0:16] + both[16:32] + both[32:48]
    pick = iota((16, 2048), 0) == iota((16, 2048), 1) % 16
    fe = jnp.where(pick, both[48:64] + both[64:80] + both[80:96], 0.0).sum(0, keepdims=True)
    fm = jnp.where(pick, both[96:112], 0.0).sum(0, keepdims=True)
    occ = 1.0 / (jnp.exp(fe * (1.0 / KT)) + 1.0)
    r.fa[pl.ds(pl.multiple_of(s * 8, 8), 8)] = jnp.concatenate([fe, fm, occ, jnp.zeros((5, 2048), F32)], 0)


def regroup_rows(r, tiles):
    cols = []
    for c in range(2):
        rows = []
        for hi in range(2):
            t = tiles[c][hi]
            rows += swap_groups([t[k * 16:k * 16 + 16] for k in range(8)])
        cols.append(jnp.concatenate(rows, 0))
    return dot(r.mix[...], jnp.concatenate(cols, 1)).astype(BF16)


def rotations(r, s, step):
    for w, left, at in ((0, r.eye[0:128, 0:128], s), (1, r.turned[...], partner_set(s, step))):
        points = dot_nt(left, r.u[at]).astype(BF16)
        out = regroup_rows(r, [[points[:, c * 256 + hi * 128:c * 256 + hi * 128 + 128] for hi in range(2)]
                               for c in range(2)])
        r.xs[w, s, 0] = out[:, 0:128]
        r.xs[w, s, 1] = out[:, 128:256]
        r.xs[w, s, 2] = -out[:, 128:256]


def vertex(r, m, half, onsite):
    rows = r.ph[half * 4:half * 4 + 4].reshape(1024, 2048)
    v = dot(rows, r.g[m].reshape(2048, 256))
    for s in range(4):
        for c in range(2):
            at = s * 256 + c * 128
            r.v[half, at:at + 128] = (v[at:at + 128] + onsite[c]).astype(BF16)


def regroup_vertex(r, m, half):
    for s in range(4):
        parts = [[r.v[half, s * 256 + c * 128:s * 256 + c * 128 + 128, hi * 128:hi * 128 + 128] for hi in range(2)]
                 for c in range(2)]
        r.t1[half * 4 + s, m] = regroup_rows(r, parts)


def block_matrix(r, w, s, o, sign):
    rows = slice(o * 16, o * 16 + 16)
    d = r.diag[...]
    wr, wi, wn = [jnp.concatenate([r.xs[w, s, i, rows]] * 8, 0) * d for i in range(3)]
    if sign > 0:
        return jnp.concatenate([jnp.concatenate([wr, wi], 1), jnp.concatenate([wn, wr], 1)], 0)
    return jnp.concatenate([jnp.concatenate([wr, wn], 1), jnp.concatenate([wi, wr], 1)], 0)


def self_energy(r, s, bose, phonon):
    for o in range(16):
        rows = slice(o * 16, o * 16 + 16)
        left = jnp.concatenate([r.t1[s, m, rows] for m in range(3)], 0)
        mixed = dot(left, block_matrix(r, 0, s, o, 1)).astype(BF16)
        inner = slice(o % 8 * 16, o % 8 * 16 + 16)
        for m in range(3):
            r.t2[o // 8 * 3 + m, inner] = mixed[m * 16:m * 16 + 16]
    for i in range(6):
        r.t3[i] = dot_nt(r.eye[...], r.t2[i]).astype(BF16)
    for o in range(16):
        hi, lo = o // 2, o % 2
        left = jnp.concatenate(
            [jnp.concatenate([r.t3[lo * 3 + m, c * 128 + hi * 16:c * 128 + hi * 16 + 16] for c in range(2)], 1)
             for m in range(3)], 0)
        bloch = dot(left, block_matrix(r, 1, s, o, -1))
        br, bi = bloch[:, 0:128], bloch[:, 128:256]
        strength = br * br + bi * bi
        cols = slice(o * 128, o * 128 + 128)
        eo = r.ex[pl.ds(pl.multiple_of(s * 16, 16), 16), cols]
        far = r.fa[pl.ds(pl.multiple_of(s * 8, 8), 8), cols]
        fe, fm, occ = far[0:1], far[1:2], far[2:3]
        diff = eo - fe
        re, im = 0.0, 0.0
        for m in range(3):
            em = fm * (bose[m] + occ)
            ab = fm * (bose[m] + 1.0 - occ)
            up = diff + phonon[m]
            lw = diff - phonon[m]
            du = up * up + ETA * ETA
            dl = lw * lw + ETA * ETA
            scale = strength[m * 16:m * 16 + 16] / (du * dl)
            e1 = em * dl
            a1 = ab * du
            re = re + scale * (e1 * up + a1 * lw)
            im = im + scale * (e1 + a1)
        r.sums[pl.ds(pl.multiple_of(s * 32, 32), 16), cols] = re
        r.sums[pl.ds(pl.multiple_of(s * 32 + 16, 16), 16), cols] = im * (-ETA)


def band_sum(r):
    hi, lo = pieces(r.sums[...], 2)
    return (dot_nt(hi, r.rep[...]) + dot_nt(lo, r.rep[...])) * (1.0 / 384.0)


def mode_terms(freq, froh, step, mode0):
    lane = iota((1, 256), 1)
    site = jnp.where(lane // 16 == lane % 16, 1.0, 0.0)
    onsite = [[site * froh[step, c, mode0 + m] for c in range(2)] for m in range(3)]
    phonon = [jnp.full((1, 128), freq[step, mode0 + m], F32) for m in range(3)]
    bose = [1.0 / (jnp.exp(w * (1.0 / KT)) - 1.0) for w in phonon]
    return onsite, phonon, bose


def loop(body):
    def step(s, carry):
        body(s)
        return carry
    lax.fori_loop(0, 8, step, 0)


def position():
    kp = lax.axis_index("kp")
    return lax.axis_index("grp"), kp // 8, kp // 4 % 2, kp % 4


def at(g, x, zh, y):
    return (g, x * 8 + zh * 4 + y)


def column(g, zh):
    for hop in range(1, 8):
        other = (zh * 4 + g + hop) % 8
        yield hop, other % 4, other // 4


def remote(src, dst, send, recv, device):
    return pltpu.make_async_remote_copy(src_ref=src, dst_ref=dst, send_sem=send, recv_sem=recv,
                                        device_id=device, device_id_type=MESH)


def semaphores():
    dma = pltpu.SemaphoreType.DMA
    return dict(
        in_sem=dma((6,)), near_sem=dma((2, 3)),
        z_send=dma((2, 3)), z_recv=dma((2, 3)),
        u_send=dma((8,)), u_recv=dma((8,)), e_send=dma((8,)), e_recv=dma((8,)),
        p_send=dma((2, 2, 4)), p_recv=dma((2, 2, 4)),
        g_send=dma((2, 3, 16)), g_recv=dma((2, 3, 16)),
        a_send=dma((8,)), a_recv=dma((8,)), b_send=dma((32,)), b_recv=dma((32,)),
    )


def io_shapes():
    vm = pltpu.VMEM
    return dict(
        uin=vm((512, 128), F32), en=vm((16, 128), F32), mask=vm((16, 128), jnp.int32),
        lat=vm((3, 1024), jnp.int32), kq=vm((2, 128), jnp.int32), irr=vm((1, 128), jnp.int32),
        part=vm((8, 32, 128), F32), got=vm((8, 32, 128), F32),
        stars=vm((512, 128), F32), blocks=vm((32, 16, 128), F32),
    )


def kernel(names, g_ref, u_ref, en_ref, mask_ref, lat_ref, kq_ref, irr_ref, freq, froh,
           sigma_ref, star_ref, *scratch):
    r = SimpleNamespace(**dict(zip(names, scratch)))
    g, x, zh, y = position()
    me = x * 8 + zh * 4 + y
    mine = zh * 4 + g
    step, mode0 = zh, g * 3

    def first(s):
        return (x * 8 + y) * 128 + lax.rem(s, 4) * 4096 + s // 4 * 512

    loads = [pltpu.make_async_copy(src, dst, r.in_sem.at[i]) for i, (src, dst) in enumerate(
        ((u_ref, r.uin), (en_ref, r.en), (mask_ref, r.mask), (lat_ref, r.lat), (kq_ref, r.kq), (irr_ref, r.irr)))]
    for copy in loads:
        copy.start()

    barrier = pltpu.get_barrier_semaphore()
    friends = [at(g2, x, zh2, y) for _, g2, zh2 in column(g, zh)] + [(g, (me + hop) % 32) for hop in range(1, 32)]
    for device in friends:
        pl.semaphore_signal(barrier, inc=1, device_id=device, device_id_type=MESH)

    def part(at_step, triple, c, m):
        return g_ref.at[at_step, :, pl.ds(pl.multiple_of(c * 3072 + triple * 768 + m * 256, 256), 256)]

    near = []
    for c in range(2):
        for m in range(3):
            near.append(pltpu.make_async_copy(part(zh, g, c, m), r.g.at[m, c, x, zh, y], r.near_sem.at[c, m]))
            near[-1].start()
    pl.semaphore_wait(barrier, len(friends))

    pz, pg = 1 - zh, (g + 2) % 4
    far = []
    for c in range(2):
        for m in range(3):
            far.append(remote(part(pz, pg, c, m), r.g.at[m, c, x, zh, y], r.z_send.at[c, m], r.z_recv.at[c, m],
                              at(pg, x, pz, y)))
            far[-1].start()
    sent = list(far)

    def go(copy):
        copy.start()
        sent.append(copy)

    def plane(hop, along_x):
        return at(g, (x + hop) % 4, zh, y) if along_x else at(g, x, zh, (y + hop) % 4)

    def first_leg(c, half, z):
        piece = r.g.at[:, c, x, z, y]
        for hop in (1, 3, 2):
            go(remote(piece, piece, r.p_send.at[c, half, hop], r.p_recv.at[c, half, hop], plane(hop, c == 0)))

    for copy in near:
        copy.wait()
    for c in range(2):
        first_leg(c, 0, zh)

    loads[0].wait()
    r.u[mine] = r.uin[...].astype(BF16)
    loads[1].wait()
    loads[2].wait()
    r.e[mine, 0:16] = r.en[...]
    r.e[mine, 16:32] = r.mask[...].astype(F32)
    small = []
    for hop, g2, zh2 in column(g, zh):
        device = at(g2, x, zh2, y)
        small.append(remote(r.u.at[mine], r.u.at[mine], r.u_send.at[hop], r.u_recv.at[hop], device))
        small.append(remote(r.e.at[mine], r.e.at[mine], r.e_send.at[hop], r.e_recv.at[hop], device))
        small[-2].start()
        small[-1].start()

    constants(r)
    loads[4].wait()
    partner_order(r, r.kq[...], step)
    loads[3].wait()
    tables(r, r.lat[...], first)
    for copy in far:
        copy.wait_recv()
    for c in range(2):
        first_leg(c, 1, 1 - zh)

    def second_leg(m, c, hop):
        xs, ys = ((x + 4 - hop) % 4, y) if c == 0 else (x, (y + 4 - hop) % 4)
        piece = r.g.at[m, c, xs, :, ys]
        for to in (1, 3, 2):
            go(remote(piece, piece, r.g_send.at[c, m, 4 * hop + to], r.g_recv.at[c, m, 4 * hop + to],
                      plane(to, c == 1)))

    for m in range(3):
        for hop in (0, 1, 3, 2):
            for c in range(2):
                if m == 0 and hop:
                    for half in range(2):
                        z = zh if half == 0 else 1 - zh
                        xs, ys = ((x + 4 - hop) % 4, y) if c == 0 else (x, (y + 4 - hop) % 4)
                        piece = r.g.at[:, c, xs, z, ys]
                        remote(piece, piece, r.p_send.at[c, half, hop], r.p_recv.at[c, half, hop],
                               plane(hop, c == 0)).wait_recv()
                second_leg(m, c, hop)

    loop(lambda s: phases(r, s, first))
    for copy in small:
        copy.wait_recv()
    sent += small
    loop(lambda s: levels(r, s, step))
    loop(lambda s: rotations(r, s, step))
    onsite, phonon, bose = mode_terms(freq, froh, step, mode0)

    def arrived(m):
        for hop in (0, 1, 3, 2):
            for to in (1, 3, 2):
                for c in range(2):
                    a, b = (hop, to) if c == 0 else (to, hop)
                    piece = r.g.at[m, c, (x + 4 - a) % 4, :, (y + 4 - b) % 4]
                    remote(piece, piece, r.g_send.at[c, m, 4 * hop + to], r.g_recv.at[c, m, 4 * hop + to],
                           plane(to, c == 1)).wait_recv()

    for m in range(3):
        arrived(m)
        vertex(r, m, 0, onsite[m])
        if m:
            regroup_vertex(r, m - 1, 1)
        vertex(r, m, 1, onsite[m])
        regroup_vertex(r, m, 0)
    regroup_vertex(r, 2, 1)
    loop(lambda s: self_energy(r, s, bose, phonon))
    total = band_sum(r)
    for s in range(8):
        r.part[s] = total[s * 32:s * 32 + 32]

    sums = []
    for hop, g2, zh2 in column(g, zh):
        sums.append(remote(r.part.at[zh2 * 4 + g2], r.got.at[hop], r.a_send.at[hop], r.a_recv.at[hop],
                           at(g2, x, zh2, y)))
        go(sums[-1])
    loads[5].wait()
    member = jnp.where(iota((512, 128), 0) == r.irr[...], 1.0, 0.0).astype(BF16)
    total = r.part[mine]
    for hop, copy in enumerate(sums, 1):
        copy.wait_recv()
        total = total + r.got[hop]
    sigma_ref[0] = total[0:16]
    sigma_ref[1] = total[16:32]
    columns = jnp.concatenate(pieces(total, 3) + [jnp.ones((32, 128), BF16)], 0)
    r.stars[...] = dot_nt(member, columns)
    blocks = []
    for hop in range(1, 32):
        owner = (me + hop) % 32
        blocks.append(remote(r.stars.at[pl.ds(pl.multiple_of(owner * 16, 16), 16)], r.blocks.at[hop],
                             r.b_send.at[hop], r.b_recv.at[hop], (g, owner)))
        go(blocks[-1])
    mean = r.stars[pl.ds(pl.multiple_of(me * 16, 16), 16)]
    for hop, copy in enumerate(blocks, 1):
        copy.wait_recv()
        mean = mean + r.blocks[hop]
    count = pltpu.roll(mean, 32, 1)
    mean = mean + pltpu.roll(mean, 96, 1) + pltpu.roll(mean, 64, 1)
    mean = (mean / jnp.maximum(count, 1.0)).T
    star_ref[0] = mean[0:16]
    star_ref[1] = mean[16:32]
    for copy in sent:
        copy.wait_send()


def local(g_real, lattice, u_rot, energy, band_mask, freq, froh, kq_index, irr_id):
    anywhere = pl.BlockSpec(memory_space=pl.ANY)
    scalars = pl.BlockSpec(memory_space=pltpu.SMEM)
    vm = pl.BlockSpec(memory_space=pltpu.VMEM)
    scratch = {**scratch_shapes(), **io_shapes(), **semaphores()}
    return pl.pallas_call(
        functools.partial(kernel, list(scratch)),
        out_shape=(jax.ShapeDtypeStruct((2, 16, 128), F32), jax.ShapeDtypeStruct((2, 16, 16), F32)),
        in_specs=[anywhere] * 7 + [scalars] * 2,
        out_specs=(vm, vm),
        scratch_shapes=list(scratch.values()),
        compiler_params=pltpu.CompilerParams(collective_id=0, has_side_effects=True,
                                             vmem_limit_bytes=60 * 2 ** 20),
    )(g_real, u_rot.reshape(512, 128), energy, band_mask, lattice, kq_index, irr_id.reshape(1, 128), freq, froh)


def solution(mesh):
    in_specs = (
        P(None, "kp", None),
        P(),
        P(None, None, None, ("grp", "kp")),
        P(None, ("grp", "kp")),
        P(None, ("grp", "kp")),
        P(),
        P(),
        P(),
        P(("grp", "kp")),
    )
    out_specs = (P(None, None, ("grp", "kp")), P(None, None, ("grp", "kp")))
    return jax.shard_map(local, mesh=mesh, in_specs=in_specs, out_specs=out_specs, check_vma=False)
```

time: 649 us -> 75.7 us (0.12)
  local copies, waits for them, and re-layouts: 262 us -> 1.94 us
  waiting for transfers between devices: 196 us -> 0 us
  blocking collectives: 91.7 us -> 0 us
  Pallas kernels: 0 us -> 72.9 us
  other arithmetic: 55.6 us -> 0 us
  between operations: 18 us -> 0.65 us
  matrix products: 14.6 us -> 0 us
    unnamed x319 -> x4, local copies, waits for them, and re-layouts: 110 us -> 1.94 us
    all_gather x1 -> x0, waiting for transfers between devices: 108 us -> none  [local(): gathered = lax.all_gather(g_real, 'kp', axis=1, tiled=True)]
    unnamed x1 -> x0, blocking collectives: 91.7 us -> none
    reduce_scatter x1 -> x0, waiting for transfers between devices: 88.3 us -> none  [local(): lax.psum_scatter(partial_sums, 'kp', scatter_dimension=0, tiled=True)]
    pallas_call x0 -> x1, Pallas kernels: none -> 72.9 us  [local(): pl.pallas_call(functools.partial(kernel, list(scratch)), out_shape=(jax.S...]
    slice x16 -> x0, local copies, waits for them, and re-layouts: 71.9 us -> none  [the longest x1 47.1 us: local(): vertex = fourier(gathered[step], phases)]
    mul x136 -> x0, local copies, waits for them, and re-layouts: 69.1 us -> none  [the longest x68 64.8 us: contribution(): bloch_re = bloch_re + rot_re * part_re + rot_im * part_im]
    reduce_sum x3 -> x0, other arithmetic: 21.4 us -> none  [the longest x2 21.2 us: contribution(): return jnp.stack([real_part.sum((0, 1)), imag_part.sum((0, 1))])]
  transfers between devices with their start and end apart: 6 -> 0, of which waited for: 2 -> 0; matrix products, arithmetic and copies ran while one was open for 15% -> 0% of each run, Pallas kernels for 0% -> 0%
where the time goes in v2:
time: 75.7 us; the launch traced here: 75.5 us
  Pallas kernels  72.9 us (96%)
  local copies, waits for them, and re-layouts  1.94 us (3%)
    pallas_call x1, Pallas kernels, local(): pl.pallas_call(functools.partial(kernel, list(scratch)), out_shape=(jax.S...  72.9 us
    unnamed x4, local copies, waits for them, and re-layouts  1.94 us

profile of v2, /device:TPU:0, one launch (start us, length us, event | category | flops | bytes accessed | tf_op | source)
XLA Modules:
  0.0 75.5 jit_solution(11501841264058605759)
XLA Ops:
  0.6 72.9 %shard_map.104 = (f32[2,16,128]{2,1,0:T(8,128)}, f32[2,16,16]{2,1,0:T(8,128)}) custom-call(bf16[2,32,6144]{2,1,0:T(8,128)(2,1)} %g_ref.1, f32[512,128]{1,0:T(8,128)} %bitcast.2, f32[16,128]{1,0:T(8,128)} %en_ref.1, s32[16,128]{1,0:T(8,128)} %mask_ref.1, s32[3,1024]{1,0:T(4,128)} %lat_ref.1, s32[2,128]{1,0:T(2,128)} %kq_ref.1, s32[1,128]{1,0:T(1,128)} %bitcast.3, ...), custom_call_target="tpu_custom_call" | custom-call | tf_op jit(solution)/shard_map/pallas_call | solution.py:485
  73.5 0.0 copy-start
  73.5 1.3 %copy.13 = f32[2,16,128]{2,1,0:T(8,128)} copy(f32[2,16,128]{2,1,0:T(8,128)} %get-tuple-element.4) | data formatting | bytes 32768
  74.9 0.0 copy-done
  74.9 0.6 copy.14
Async XLA Ops:
  73.5 1.3 %copy-start = (f32[2,16,16]{2,1,0:T(8,128)S(1)}, f32[2,16,16]{2,1,0:T(8,128)}, u32[]{:S(2)}) copy-start(f32[2,16,16]{2,1,0:T(8,128)} %get-tuple-element.5) | copy-start | bytes 6148

commit v3 on v2

--- a/solution.py
+++ b/solution.py
@@ -50,6 +50,11 @@
 
 def iota(shape, axis):
     return lax.broadcasted_iota(jnp.int32, shape, axis)
+
+
+def together(work):
+    while work:
+        work = [w for w in work if next(w, work) is not work]
 
 
 def swap_groups(parts):
@@ -75,13 +80,13 @@
         bc=vm((128, 1024), F32), bs=vm((128, 1024), F32),
         ph=vm((8, 256, 2048), BF16),
         v=vm((2, 1024, 256), BF16),
-        xs=vm((2, 8, 3, 256, 128), BF16),
+        xs=vm((2, 8, 2, 256, 128), BF16),
         t1=vm((8, 3, 256, 256), BF16),
-        t2=vm((6, 128, 256), BF16),
-        t3=vm((6, 256, 128), BF16),
+        t2=vm((2, 6, 128, 256), BF16),
+        t3=vm((2, 6, 256, 128), BF16),
         ex=vm((128, 2048), F32), fa=vm((64, 2048), F32),
         sums=vm((256, 2048), F32),
-        rep=vm((128, 2048), BF16), diag=vm((128, 128), BF16), eye=vm((256, 256), BF16),
+        rep=vm((128, 2048), BF16), rept=vm((2048, 128), BF16), diag=vm((128, 128), BF16), eye=vm((128, 128), BF16),
         mix=vm((256, 256), BF16), perm=vm((128, 128), BF16), turned=vm((128, 128), BF16),
     )
 
@@ -89,10 +94,12 @@
 def constants(r):
     rr, rl = iota((128, 2048), 0), iota((128, 2048), 1)
     r.rep[...] = jnp.where(rl // 16 == rr, 1.0, 0.0).astype(BF16)
+    rr, rl = iota((2048, 128), 0), iota((2048, 128), 1)
+    r.rept[...] = jnp.where(rr // 16 == rl, 1.0, 0.0).astype(BF16)
     sr, sl = iota((128, 128), 0), iota((128, 128), 1)
     r.diag[...] = jnp.where(sr // 16 == sl // 16, 1.0, 0.0).astype(BF16)
     br, bl = iota((256, 256), 0), iota((256, 256), 1)
-    r.eye[...] = jnp.where(br == bl, 1.0, 0.0).astype(BF16)
+    r.eye[...] = jnp.where(sr == sl, 1.0, 0.0).astype(BF16)
     r.mix[...] = jnp.where((br // 16 == bl % 16) & (br % 16 == bl // 16), 1.0, 0.0).astype(BF16)
 
 
@@ -155,7 +162,9 @@
     far = partner_set(s, step)
     far_e = pieces(r.e[far, 0:16], 3) + [r.e[far, 16:32].astype(BF16)]
     moved = dot_nt(jnp.concatenate(far_e, 0), r.perm[...]).astype(BF16)
+    yield
     both = dot(jnp.concatenate(own + [moved], 0), r.rep[...])
+    yield
     r.ex[pl.ds(pl.multiple_of(s * 16, 16), 16)] = both[0:16] + both[16:32] + both[32:48]
     pick = iota((16, 2048), 0) == iota((16, 2048), 1) % 16
     fe = jnp.where(pick, both[48:64] + both[64:80] + both[80:96], 0.0).sum(0, keepdims=True)
@@ -164,7 +173,7 @@
     r.fa[pl.ds(pl.multiple_of(s * 8, 8), 8)] = jnp.concatenate([fe, fm, occ, jnp.zeros((5, 2048), F32)], 0)
 
 
-def regroup_rows(r, tiles):
+def regroup_columns(tiles):
     cols = []
     for c in range(2):
         rows = []
@@ -172,17 +181,23 @@
             t = tiles[c][hi]
             rows += swap_groups([t[k * 16:k * 16 + 16] for k in range(8)])
         cols.append(jnp.concatenate(rows, 0))
-    return dot(r.mix[...], jnp.concatenate(cols, 1)).astype(BF16)
-
-
-def rotations(r, s, step):
-    for w, left, at in ((0, r.eye[0:128, 0:128], s), (1, r.turned[...], partner_set(s, step))):
-        points = dot_nt(left, r.u[at]).astype(BF16)
-        out = regroup_rows(r, [[points[:, c * 256 + hi * 128:c * 256 + hi * 128 + 128] for hi in range(2)]
-                               for c in range(2)])
-        r.xs[w, s, 0] = out[:, 0:128]
-        r.xs[w, s, 1] = out[:, 128:256]
-        r.xs[w, s, 2] = -out[:, 128:256]
+    return jnp.concatenate(cols, 1)
+
+
+def regroup_rows(r, tiles):
+    return dot(r.mix[...], regroup_columns(tiles)).astype(BF16)
+
+
+def rotations(r, w, s, step):
+    left, at = (r.eye[...], s) if w == 0 else (r.turned[...], partner_set(s, step))
+    points = dot_nt(left, r.u[at]).astype(BF16)
+    yield
+    cols = regroup_columns([[points[:, c * 256 + hi * 128:c * 256 + hi * 128 + 128] for hi in range(2)]
+                            for c in range(2)])
+    yield
+    out = dot(r.mix[...], cols).astype(BF16)
+    r.xs[w, s, 0] = out[:, 0:128]
+    r.xs[w, s, 1] = out[:, 128:256]
 
 
 def vertex(r, m, half, onsite):
@@ -201,32 +216,34 @@
         r.t1[half * 4 + s, m] = regroup_rows(r, parts)
 
 
-def block_matrix(r, w, s, o, sign):
+def block_matrix(r, w, s, o):
     rows = slice(o * 16, o * 16 + 16)
     d = r.diag[...]
-    wr, wi, wn = [jnp.concatenate([r.xs[w, s, i, rows]] * 8, 0) * d for i in range(3)]
-    if sign > 0:
-        return jnp.concatenate([jnp.concatenate([wr, wi], 1), jnp.concatenate([wn, wr], 1)], 0)
-    return jnp.concatenate([jnp.concatenate([wr, wn], 1), jnp.concatenate([wi, wr], 1)], 0)
-
-
-def self_energy(r, s, bose, phonon):
+    return jnp.concatenate([jnp.concatenate([r.xs[w, s, i, rows]] * 8, 0) * d for i in range(2)], 1)
+
+
+def self_energy(r, s, lane, bose, phonon):
     for o in range(16):
         rows = slice(o * 16, o * 16 + 16)
-        left = jnp.concatenate([r.t1[s, m, rows] for m in range(3)], 0)
-        mixed = dot(left, block_matrix(r, 0, s, o, 1)).astype(BF16)
+        left = jnp.concatenate([r.t1[s, m, rows, c * 128:c * 128 + 128] for c in range(2) for m in range(3)], 0)
+        both = dot(left, block_matrix(r, 0, s, o))
+        re = (both[0:48, 0:128] - both[48:96, 128:256]).astype(BF16)
+        im = (both[0:48, 128:256] + both[48:96, 0:128]).astype(BF16)
         inner = slice(o % 8 * 16, o % 8 * 16 + 16)
         for m in range(3):
-            r.t2[o // 8 * 3 + m, inner] = mixed[m * 16:m * 16 + 16]
+            r.t2[lane, o // 8 * 3 + m, inner, 0:128] = re[m * 16:m * 16 + 16]
+            r.t2[lane, o // 8 * 3 + m, inner, 128:256] = im[m * 16:m * 16 + 16]
+    yield
     for i in range(6):
-        r.t3[i] = dot_nt(r.eye[...], r.t2[i]).astype(BF16)
+        r.t3[lane, i] = r.t2[lane, i].T
+    yield
     for o in range(16):
         hi, lo = o // 2, o % 2
-        left = jnp.concatenate(
-            [jnp.concatenate([r.t3[lo * 3 + m, c * 128 + hi * 16:c * 128 + hi * 16 + 16] for c in range(2)], 1)
-             for m in range(3)], 0)
-        bloch = dot(left, block_matrix(r, 1, s, o, -1))
-        br, bi = bloch[:, 0:128], bloch[:, 128:256]
+        left = jnp.concatenate([r.t3[lane, lo * 3 + m, c * 128 + hi * 16:c * 128 + hi * 16 + 16]
+                                for c in range(2) for m in range(3)], 0)
+        both = dot(left, block_matrix(r, 1, s, o))
+        br = both[0:48, 0:128] + both[48:96, 128:256]
+        bi = both[48:96, 0:128] - both[0:48, 128:256]
         strength = br * br + bi * bi
         cols = slice(o * 128, o * 128 + 128)
         eo = r.ex[pl.ds(pl.multiple_of(s * 16, 16), 16), cols]
@@ -252,23 +269,28 @@
 
 def band_sum(r):
     hi, lo = pieces(r.sums[...], 2)
-    return (dot_nt(hi, r.rep[...]) + dot_nt(lo, r.rep[...])) * (1.0 / 384.0)
+    return (dot(hi, r.rept[...]) + dot(lo, r.rept[...])) * (1.0 / 384.0)
 
 
 def mode_terms(freq, froh, step, mode0):
     lane = iota((1, 256), 1)
     site = jnp.where(lane // 16 == lane % 16, 1.0, 0.0)
-    onsite = [[site * froh[step, c, mode0 + m] for c in range(2)] for m in range(3)]
-    phonon = [jnp.full((1, 128), freq[step, mode0 + m], F32) for m in range(3)]
+
+    def pick(rows, m):
+        row = jnp.where(step == 0, rows[0:1], rows[1:2])
+        return jnp.where(iota((1, 12), 1) == mode0 + m, row, 0.0).sum(1, keepdims=True)
+
+    onsite = [[site * pick(froh[:, c], m) for c in range(2)] for m in range(3)]
+    phonon = [jnp.broadcast_to(pick(freq, m), (1, 128)) for m in range(3)]
     bose = [1.0 / (jnp.exp(w * (1.0 / KT)) - 1.0) for w in phonon]
     return onsite, phonon, bose
 
 
-def loop(body):
+def loop(body, count=8):
     def step(s, carry):
         body(s)
         return carry
-    lax.fori_loop(0, 8, step, 0)
+    lax.fori_loop(0, count, step, 0)
 
 
 def position():
@@ -294,12 +316,12 @@
 def semaphores():
     dma = pltpu.SemaphoreType.DMA
     return dict(
-        in_sem=dma((6,)), near_sem=dma((2, 3)),
+        in_sem=dma((8,)), near_sem=dma((2, 3)),
         z_send=dma((2, 3)), z_recv=dma((2, 3)),
         u_send=dma((8,)), u_recv=dma((8,)), e_send=dma((8,)), e_recv=dma((8,)),
         p_send=dma((2, 2, 4)), p_recv=dma((2, 2, 4)),
         g_send=dma((2, 3, 16)), g_recv=dma((2, 3, 16)),
-        a_send=dma((8,)), a_recv=dma((8,)), b_send=dma((32,)), b_recv=dma((32,)),
+        a_send=dma((8,)), a_recv=dma((8,)), b_send=dma((17,)), b_recv=dma((17,)),
     )
 
 
@@ -309,15 +331,16 @@
         uin=vm((512, 128), F32), en=vm((16, 128), F32), mask=vm((16, 128), jnp.int32),
         lat=vm((3, 1024), jnp.int32), kq=vm((2, 128), jnp.int32), irr=vm((1, 128), jnp.int32),
         part=vm((8, 32, 128), F32), got=vm((8, 32, 128), F32),
-        stars=vm((512, 128), F32), blocks=vm((32, 16, 128), F32),
+        stars=vm((4, 2, 4, 16, 128), F32), blocks=vm((16, 2, 16, 128), F32),
+        pairs=vm((2, 16, 128), F32), other=vm((16, 128), F32),
+        freq=vm((2, 12), F32), froh=vm((2, 2, 12), F32),
     )
 
 
-def kernel(names, g_ref, u_ref, en_ref, mask_ref, lat_ref, kq_ref, irr_ref, freq, froh,
+def kernel(names, g_ref, u_ref, en_ref, mask_ref, lat_ref, kq_ref, irr_ref, freq_ref, froh_ref,
            sigma_ref, star_ref, *scratch):
     r = SimpleNamespace(**dict(zip(names, scratch)))
     g, x, zh, y = position()
-    me = x * 8 + zh * 4 + y
     mine = zh * 4 + g
     step, mode0 = zh, g * 3
 
@@ -325,12 +348,14 @@
         return (x * 8 + y) * 128 + lax.rem(s, 4) * 4096 + s // 4 * 512
 
     loads = [pltpu.make_async_copy(src, dst, r.in_sem.at[i]) for i, (src, dst) in enumerate(
-        ((u_ref, r.uin), (en_ref, r.en), (mask_ref, r.mask), (lat_ref, r.lat), (kq_ref, r.kq), (irr_ref, r.irr)))]
+        ((u_ref, r.uin), (en_ref, r.en), (mask_ref, r.mask), (lat_ref, r.lat), (kq_ref, r.kq), (irr_ref, r.irr),
+         (freq_ref, r.freq), (froh_ref, r.froh)))]
     for copy in loads:
         copy.start()
 
     barrier = pltpu.get_barrier_semaphore()
-    friends = [at(g2, x, zh2, y) for _, g2, zh2 in column(g, zh)] + [(g, (me + hop) % 32) for hop in range(1, 32)]
+    friends = [at(g2, x, zh2, y) for _, g2, zh2 in column(g, zh)] + [
+        at(g, (x + i // 4) % 4, zh, (y + i % 4) % 4) for i in range(1, 16)]
     for device in friends:
         pl.semaphore_signal(barrier, inc=1, device_id=device, device_id_type=MESH)
 
@@ -365,25 +390,30 @@
         for hop in (1, 3, 2):
             go(remote(piece, piece, r.p_send.at[c, half, hop], r.p_recv.at[c, half, hop], plane(hop, c == 0)))
 
+    chip, sibling = mine // 2, at(g // 2 * 2 + 1 - g % 2, x, zh, y)
+
+    def share(slot, sem, device):
+        for buf, send, recv in ((r.u, r.u_send, r.u_recv), (r.e, r.e_send, r.e_recv)):
+            go(remote(buf.at[slot], buf.at[slot], send.at[sem], recv.at[sem], device))
+
+    def shared(slot, sem):
+        for buf, send, recv in ((r.u, r.u_send, r.u_recv), (r.e, r.e_send, r.e_recv)):
+            remote(buf.at[slot], buf.at[slot], send.at[sem], recv.at[sem], sibling).wait_recv()
+
+    for i in range(3):
+        loads[i].wait()
+    r.u[mine] = r.uin[...].astype(BF16)
+    r.e[mine, 0:16] = r.en[...]
+    r.e[mine, 16:32] = r.mask[...].astype(F32)
+    for hop in (1, 3, 2):
+        there = (chip + hop) % 4
+        share(mine, hop, at(there % 2 * 2 + g % 2, x, there // 2, y))
+    share(mine, 0, sibling)
+
     for copy in near:
         copy.wait()
     for c in range(2):
         first_leg(c, 0, zh)
-
-    loads[0].wait()
-    r.u[mine] = r.uin[...].astype(BF16)
-    loads[1].wait()
-    loads[2].wait()
-    r.e[mine, 0:16] = r.en[...]
-    r.e[mine, 16:32] = r.mask[...].astype(F32)
-    small = []
-    for hop, g2, zh2 in column(g, zh):
-        device = at(g2, x, zh2, y)
-        small.append(remote(r.u.at[mine], r.u.at[mine], r.u_send.at[hop], r.u_recv.at[hop], device))
-        small.append(remote(r.e.at[mine], r.e.at[mine], r.e_send.at[hop], r.e_recv.at[hop], device))
-        small[-2].start()
-        small[-1].start()
-
     constants(r)
     loads[4].wait()
     partner_order(r, r.kq[...], step)
@@ -393,6 +423,7 @@
         copy.wait_recv()
     for c in range(2):
         first_leg(c, 1, 1 - zh)
+    loop(lambda s: phases(r, s, first))
 
     def second_leg(m, c, hop):
         xs, ys = ((x + 4 - hop) % 4, y) if c == 0 else (x, (y + 4 - hop) % 4)
@@ -413,13 +444,17 @@
                                plane(hop, c == 0)).wait_recv()
                 second_leg(m, c, hop)
 
-    loop(lambda s: phases(r, s, first))
-    for copy in small:
-        copy.wait_recv()
-    sent += small
-    loop(lambda s: levels(r, s, step))
-    loop(lambda s: rotations(r, s, step))
-    onsite, phonon, bose = mode_terms(freq, froh, step, mode0)
+    for hop in (1, 3, 2):
+        shared((chip + 4 - hop) % 4 * 2 + g % 2, hop)
+        share((chip + 4 - hop) % 4 * 2 + g % 2, 4 + hop, sibling)
+    shared(chip * 2 + 1 - g % 2, 0)
+    for hop in (1, 3, 2):
+        shared((chip + 4 - hop) % 4 * 2 + 1 - g % 2, 4 + hop)
+    loop(lambda i: together([levels(r, i * 4 + q, step) for q in range(4)]), 2)
+    loop(lambda i: together([rotations(r, w, i * 4 + q, step) for q in range(4) for w in range(2)]), 2)
+    loads[6].wait()
+    loads[7].wait()
+    onsite, phonon, bose = mode_terms(r.freq[...], r.froh[...], step, mode0)
 
     def arrived(m):
         for hop in (0, 1, 3, 2):
@@ -438,7 +473,7 @@
         vertex(r, m, 1, onsite[m])
         regroup_vertex(r, m, 0)
     regroup_vertex(r, 2, 1)
-    loop(lambda s: self_energy(r, s, bose, phonon))
+    loop(lambda i: together([self_energy(r, 2 * i + q, q, bose, phonon) for q in range(2)]), 4)
     total = band_sum(r)
     for s in range(8):
         r.part[s] = total[s * 32:s * 32 + 32]
@@ -457,17 +492,23 @@
     sigma_ref[0] = total[0:16]
     sigma_ref[1] = total[16:32]
     columns = jnp.concatenate(pieces(total, 3) + [jnp.ones((32, 128), BF16)], 0)
-    r.stars[...] = dot_nt(member, columns)
+    r.stars[...] = dot_nt(member, columns).reshape(4, 2, 4, 16, 128)
     blocks = []
-    for hop in range(1, 32):
-        owner = (me + hop) % 32
-        blocks.append(remote(r.stars.at[pl.ds(pl.multiple_of(owner * 16, 16), 16)], r.blocks.at[hop],
-                             r.b_send.at[hop], r.b_recv.at[hop], (g, owner)))
+    for i in range(1, 16):
+        xs, ys = (x + i // 4) % 4, (y + i % 4) % 4
+        blocks.append(remote(r.stars.at[xs, :, ys], r.blocks.at[i], r.b_send.at[i], r.b_recv.at[i],
+                             at(g, xs, zh, ys)))
         go(blocks[-1])
-    mean = r.stars[pl.ds(pl.multiple_of(me * 16, 16), 16)]
-    for hop, copy in enumerate(blocks, 1):
+    mean = r.stars[x, :, y]
+    for i, copy in enumerate(blocks, 1):
         copy.wait_recv()
-        mean = mean + r.blocks[hop]
+        mean = mean + r.blocks[i]
+    r.pairs[...] = mean
+    last = remote(r.pairs.at[1 - zh], r.other, r.b_send.at[16], r.b_recv.at[16], at(g, x, 1 - zh, y))
+    go(last)
+    mean = r.pairs[zh]
+    last.wait_recv()
+    mean = mean + r.other[...]
     count = pltpu.roll(mean, 32, 1)
     mean = mean + pltpu.roll(mean, 96, 1) + pltpu.roll(mean, 64, 1)
     mean = (mean / jnp.maximum(count, 1.0)).T
@@ -479,13 +520,12 @@
 
 def local(g_real, lattice, u_rot, energy, band_mask, freq, froh, kq_index, irr_id):
     anywhere = pl.BlockSpec(memory_space=pl.ANY)
-    scalars = pl.BlockSpec(memory_space=pltpu.SMEM)
     vm = pl.BlockSpec(memory_space=pltpu.VMEM)
     scratch = {**scratch_shapes(), **io_shapes(), **semaphores()}
     return pl.pallas_call(
         functools.partial(kernel, list(scratch)),
         out_shape=(jax.ShapeDtypeStruct((2, 16, 128), F32), jax.ShapeDtypeStruct((2, 16, 16), F32)),
-        in_specs=[anywhere] * 7 + [scalars] * 2,
+        in_specs=[anywhere] * 9,
         out_specs=(vm, vm),
         scratch_shapes=list(scratch.values()),
         compiler_params=pltpu.CompilerParams(collective_id=0, has_side_effects=True,

time: 75.7 us -> 66.2 us (0.87)
  Pallas kernels: 72.9 us -> 63.5 us
    pallas_call x1, Pallas kernels: 72.9 us -> 63.5 us  [local(): pl.pallas_call(functools.partial(kernel, list(scratch)), out_shape=(jax.S...]
where the time goes in v3:
time: 66.2 us; the launch traced here: 66.1 us
  Pallas kernels  63.5 us (96%)
  local copies, waits for them, and re-layouts  1.94 us (3%)
    pallas_call x1, Pallas kernels, local(): pl.pallas_call(functools.partial(kernel, list(scratch)), out_shape=(jax.S...  63.5 us
    unnamed x4, local copies, waits for them, and re-layouts  1.94 us

profile of v3, /device:TPU:0, one launch (start us, length us, event | category | flops | bytes accessed | tf_op | source)
XLA Modules:
  0.0 66.1 jit_solution(12123708376229650886)
XLA Ops:
  0.6 63.5 %shard_map.104 = (f32[2,16,128]{2,1,0:T(8,128)}, f32[2,16,16]{2,1,0:T(8,128)}) custom-call(bf16[2,32,6144]{2,1,0:T(8,128)(2,1)} %g_ref.1, f32[512,128]{1,0:T(8,128)} %bitcast.2, f32[16,128]{1,0:T(8,128)} %en_ref.1, s32[16,128]{1,0:T(8,128)} %mask_ref.1, s32[3,1024]{1,0:T(4,128)} %lat_ref.1, s32[2,128]{1,0:T(2,128)} %kq_ref.1, s32[1,128]{1,0:T(1,128)} %bitcast.3, ...), custom_call_target="tpu_custom_call" | custom-call | tf_op jit(solution)/shard_map/pallas_call | solution.py:525
  64.1 0.0 copy-start
  64.1 1.3 %copy.13 = f32[2,16,128]{2,1,0:T(8,128)} copy(f32[2,16,128]{2,1,0:T(8,128)} %get-tuple-element.4) | data formatting | bytes 32768
  65.4 0.0 copy-done
  65.4 0.6 copy.14
Async XLA Ops:
  64.1 1.3 %copy-start = (f32[2,16,16]{2,1,0:T(8,128)S(1)}, f32[2,16,16]{2,1,0:T(8,128)}, u32[]{:S(2)}) copy-start(f32[2,16,16]{2,1,0:T(8,128)} %get-tuple-element.5) | copy-start | bytes 6148

commit v4 on v3

--- a/solution.py
+++ b/solution.py
@@ -316,12 +316,8 @@
 def semaphores():
     dma = pltpu.SemaphoreType.DMA
     return dict(
-        in_sem=dma((8,)), near_sem=dma((2, 3)),
-        z_send=dma((2, 3)), z_recv=dma((2, 3)),
-        u_send=dma((8,)), u_recv=dma((8,)), e_send=dma((8,)), e_recv=dma((8,)),
-        p_send=dma((2, 2, 4)), p_recv=dma((2, 2, 4)),
-        g_send=dma((2, 3, 16)), g_recv=dma((2, 3, 16)),
-        a_send=dma((8,)), a_recv=dma((8,)), b_send=dma((17,)), b_recv=dma((17,)),
+        in_sem=dma((8,)), near_sem=dma((1,)), z_sem=dma((2,)), p_sem=dma((2,)), g_send=dma((1,)), g_recv=dma((3,)),
+        u_send=dma((1,)), u_recv=dma((4,)), e_send=dma((1,)), e_recv=dma((4,)), a_sem=dma((2,)), b_sem=dma((2,)),
     )
 
 
@@ -331,8 +327,7 @@
         uin=vm((512, 128), F32), en=vm((16, 128), F32), mask=vm((16, 128), jnp.int32),
         lat=vm((3, 1024), jnp.int32), kq=vm((2, 128), jnp.int32), irr=vm((1, 128), jnp.int32),
         part=vm((8, 32, 128), F32), got=vm((8, 32, 128), F32),
-        stars=vm((4, 2, 4, 16, 128), F32), blocks=vm((16, 2, 16, 128), F32),
-        pairs=vm((2, 16, 128), F32), other=vm((16, 128), F32),
+        stars=vm((512, 128), F32), blocks=vm((32, 16, 128), F32),
         freq=vm((2, 12), F32), froh=vm((2, 2, 12), F32),
     )
 
@@ -341,6 +336,7 @@
            sigma_ref, star_ref, *scratch):
     r = SimpleNamespace(**dict(zip(names, scratch)))
     g, x, zh, y = position()
+    me = x * 8 + zh * 4 + y
     mine = zh * 4 + g
     step, mode0 = zh, g * 3
 
@@ -354,51 +350,43 @@
         copy.start()
 
     barrier = pltpu.get_barrier_semaphore()
-    friends = [at(g2, x, zh2, y) for _, g2, zh2 in column(g, zh)] + [
-        at(g, (x + i // 4) % 4, zh, (y + i % 4) % 4) for i in range(1, 16)]
+    friends = [at(g2, x, zh2, y) for _, g2, zh2 in column(g, zh)] + [(g, (me + hop) % 32) for hop in range(1, 32)]
     for device in friends:
         pl.semaphore_signal(barrier, inc=1, device_id=device, device_id_type=MESH)
 
     def part(at_step, triple, c, m):
         return g_ref.at[at_step, :, pl.ds(pl.multiple_of(c * 3072 + triple * 768 + m * 256, 256), 256)]
 
-    near = []
     for c in range(2):
         for m in range(3):
-            near.append(pltpu.make_async_copy(part(zh, g, c, m), r.g.at[m, c, x, zh, y], r.near_sem.at[c, m]))
-            near[-1].start()
+            pltpu.make_async_copy(part(zh, g, c, m), r.g.at[m, c, x, zh, y], r.near_sem.at[0]).start()
     pl.semaphore_wait(barrier, len(friends))
 
     pz, pg = 1 - zh, (g + 2) % 4
-    far = []
     for c in range(2):
         for m in range(3):
-            far.append(remote(part(pz, pg, c, m), r.g.at[m, c, x, zh, y], r.z_send.at[c, m], r.z_recv.at[c, m],
-                              at(pg, x, pz, y)))
-            far[-1].start()
-    sent = list(far)
-
-    def go(copy):
-        copy.start()
-        sent.append(copy)
+            remote(part(pz, pg, c, m), r.g.at[m, c, x, zh, y], r.z_sem.at[0], r.z_sem.at[1], at(pg, x, pz, y)).start()
+
+    def total(ref, sem):
+        pltpu.make_async_copy(ref, ref, sem).wait()
 
     def plane(hop, along_x):
         return at(g, (x + hop) % 4, zh, y) if along_x else at(g, x, zh, (y + hop) % 4)
 
-    def first_leg(c, half, z):
+    def first_leg(c, z):
         piece = r.g.at[:, c, x, z, y]
         for hop in (1, 3, 2):
-            go(remote(piece, piece, r.p_send.at[c, half, hop], r.p_recv.at[c, half, hop], plane(hop, c == 0)))
+            remote(piece, piece, r.p_sem.at[0], r.p_sem.at[1], plane(hop, c == 0)).start()
 
     chip, sibling = mine // 2, at(g // 2 * 2 + 1 - g % 2, x, zh, y)
 
     def share(slot, sem, device):
         for buf, send, recv in ((r.u, r.u_send, r.u_recv), (r.e, r.e_send, r.e_recv)):
-            go(remote(buf.at[slot], buf.at[slot], send.at[sem], recv.at[sem], device))
+            remote(buf.at[slot], buf.at[slot], send.at[0], recv.at[sem], device).start()
 
     def shared(slot, sem):
         for buf, send, recv in ((r.u, r.u_send, r.u_recv), (r.e, r.e_send, r.e_recv)):
-            remote(buf.at[slot], buf.at[slot], send.at[sem], recv.at[sem], sibling).wait_recv()
+            total(buf.at[slot], recv.at[sem])
 
     for i in range(3):
         loads[i].wait()
@@ -410,63 +398,45 @@
         share(mine, hop, at(there % 2 * 2 + g % 2, x, there // 2, y))
     share(mine, 0, sibling)
 
-    for copy in near:
-        copy.wait()
+    total(r.g.at[:, :, x, zh, y], r.near_sem.at[0])
     for c in range(2):
-        first_leg(c, 0, zh)
+        first_leg(c, zh)
     constants(r)
     loads[4].wait()
     partner_order(r, r.kq[...], step)
     loads[3].wait()
     tables(r, r.lat[...], first)
-    for copy in far:
-        copy.wait_recv()
+    total(r.g.at[:, :, x, pz, y], r.z_sem.at[1])
     for c in range(2):
-        first_leg(c, 1, 1 - zh)
+        first_leg(c, 1 - zh)
     loop(lambda s: phases(r, s, first))
 
     def second_leg(m, c, hop):
         xs, ys = ((x + 4 - hop) % 4, y) if c == 0 else (x, (y + 4 - hop) % 4)
         piece = r.g.at[m, c, xs, :, ys]
         for to in (1, 3, 2):
-            go(remote(piece, piece, r.g_send.at[c, m, 4 * hop + to], r.g_recv.at[c, m, 4 * hop + to],
-                      plane(to, c == 1)))
+            remote(piece, piece, r.g_send.at[0], r.g_recv.at[m], plane(to, c == 1)).start()
 
     for m in range(3):
         for hop in (0, 1, 3, 2):
             for c in range(2):
-                if m == 0 and hop:
-                    for half in range(2):
-                        z = zh if half == 0 else 1 - zh
-                        xs, ys = ((x + 4 - hop) % 4, y) if c == 0 else (x, (y + 4 - hop) % 4)
-                        piece = r.g.at[:, c, xs, z, ys]
-                        remote(piece, piece, r.p_send.at[c, half, hop], r.p_recv.at[c, half, hop],
-                               plane(hop, c == 0)).wait_recv()
+                if m == 0 and hop == 1 and c == 0:
+                    total(r.g.at[:, :, 0:3, :, 0], r.p_sem.at[1])
                 second_leg(m, c, hop)
 
     for hop in (1, 3, 2):
         shared((chip + 4 - hop) % 4 * 2 + g % 2, hop)
-        share((chip + 4 - hop) % 4 * 2 + g % 2, 4 + hop, sibling)
-    shared(chip * 2 + 1 - g % 2, 0)
-    for hop in (1, 3, 2):
-        shared((chip + 4 - hop) % 4 * 2 + 1 - g % 2, 4 + hop)
+        share((chip + 4 - hop) % 4 * 2 + g % 2, 0, sibling)
+    total(r.u.at[0:4], r.u_recv.at[0])
+    total(r.e.at[0:4], r.e_recv.at[0])
     loop(lambda i: together([levels(r, i * 4 + q, step) for q in range(4)]), 2)
     loop(lambda i: together([rotations(r, w, i * 4 + q, step) for q in range(4) for w in range(2)]), 2)
     loads[6].wait()
     loads[7].wait()
     onsite, phonon, bose = mode_terms(r.freq[...], r.froh[...], step, mode0)
 
-    def arrived(m):
-        for hop in (0, 1, 3, 2):
-            for to in (1, 3, 2):
-                for c in range(2):
-                    a, b = (hop, to) if c == 0 else (to, hop)
-                    piece = r.g.at[m, c, (x + 4 - a) % 4, :, (y + 4 - b) % 4]
-                    remote(piece, piece, r.g_send.at[c, m, 4 * hop + to], r.g_recv.at[c, m, 4 * hop + to],
-                           plane(to, c == 1)).wait_recv()
-
     for m in range(3):
-        arrived(m)
+        total(r.g.at[m, :, :, :, 0:3], r.g_recv.at[m])
         vertex(r, m, 0, onsite[m])
         if m:
             regroup_vertex(r, m - 1, 1)
@@ -474,48 +444,42 @@
         regroup_vertex(r, m, 0)
     regroup_vertex(r, 2, 1)
     loop(lambda i: together([self_energy(r, 2 * i + q, q, bose, phonon) for q in range(2)]), 4)
-    total = band_sum(r)
+    sums = band_sum(r)
     for s in range(8):
-        r.part[s] = total[s * 32:s * 32 + 32]
-
-    sums = []
+        r.part[s] = sums[s * 32:s * 32 + 32]
+
     for hop, g2, zh2 in column(g, zh):
-        sums.append(remote(r.part.at[zh2 * 4 + g2], r.got.at[hop], r.a_send.at[hop], r.a_recv.at[hop],
-                           at(g2, x, zh2, y)))
-        go(sums[-1])
+        remote(r.part.at[zh2 * 4 + g2], r.got.at[hop], r.a_sem.at[0], r.a_sem.at[1], at(g2, x, zh2, y)).start()
     loads[5].wait()
     member = jnp.where(iota((512, 128), 0) == r.irr[...], 1.0, 0.0).astype(BF16)
-    total = r.part[mine]
-    for hop, copy in enumerate(sums, 1):
-        copy.wait_recv()
-        total = total + r.got[hop]
-    sigma_ref[0] = total[0:16]
-    sigma_ref[1] = total[16:32]
-    columns = jnp.concatenate(pieces(total, 3) + [jnp.ones((32, 128), BF16)], 0)
-    r.stars[...] = dot_nt(member, columns).reshape(4, 2, 4, 16, 128)
-    blocks = []
-    for i in range(1, 16):
-        xs, ys = (x + i // 4) % 4, (y + i % 4) % 4
-        blocks.append(remote(r.stars.at[xs, :, ys], r.blocks.at[i], r.b_send.at[i], r.b_recv.at[i],
-                             at(g, xs, zh, ys)))
-        go(blocks[-1])
-    mean = r.stars[x, :, y]
-    for i, copy in enumerate(blocks, 1):
-        copy.wait_recv()
-        mean = mean + r.blocks[i]
-    r.pairs[...] = mean
-    last = remote(r.pairs.at[1 - zh], r.other, r.b_send.at[16], r.b_recv.at[16], at(g, x, 1 - zh, y))
-    go(last)
-    mean = r.pairs[zh]
-    last.wait_recv()
-    mean = mean + r.other[...]
+    total(r.got.at[1:8], r.a_sem.at[1])
+    sigma = r.part[mine]
+    for hop in range(1, 8):
+        sigma = sigma + r.got[hop]
+    sigma_ref[0] = sigma[0:16]
+    sigma_ref[1] = sigma[16:32]
+    columns = jnp.concatenate(pieces(sigma, 3) + [jnp.ones((32, 128), BF16)], 0)
+    r.stars[...] = dot_nt(member, columns)
+    for hop in range(1, 32):
+        owner = (me + hop) % 32
+        remote(r.stars.at[pl.ds(pl.multiple_of(owner * 16, 16), 16)], r.blocks.at[hop],
+               r.b_sem.at[0], r.b_sem.at[1], (g, owner)).start()
+    mean = r.stars[pl.ds(pl.multiple_of(me * 16, 16), 16)]
+    total(r.blocks.at[1:32], r.b_sem.at[1])
+    for hop in range(1, 32):
+        mean = mean + r.blocks[hop]
     count = pltpu.roll(mean, 32, 1)
     mean = mean + pltpu.roll(mean, 96, 1) + pltpu.roll(mean, 64, 1)
     mean = (mean / jnp.maximum(count, 1.0)).T
     star_ref[0] = mean[0:16]
     star_ref[1] = mean[16:32]
-    for copy in sent:
-        copy.wait_send()
+    total(r.g.at[:, :, x, zh, y], r.z_sem.at[0])
+    total(r.g.at[:, :, 0:3, :, 0], r.p_sem.at[0])
+    total(r.g.at[:, :, :, :, 0:3], r.g_send.at[0])
+    total(r.u.at[0:7], r.u_send.at[0])
+    total(r.e.at[0:7], r.e_send.at[0])
+    total(r.part.at[0:7], r.a_sem.at[0])
+    total(r.blocks.at[1:32], r.b_sem.at[0])
 
 
 def local(g_real, lattice, u_rot, energy, band_mask, freq, froh, kq_index, irr_id):

time: 66.2 us -> 61.1 us (0.923)
  Pallas kernels: 63.5 us -> 58.3 us
    pallas_call x1, Pallas kernels: 63.5 us -> 58.3 us  [local(): pl.pallas_call(functools.partial(kernel, list(scratch)), out_shape=(jax.S...]
where the time goes in v4:
time: 61.1 us; the launch traced here: 60.9 us
  Pallas kernels  58.3 us (95%)
  local copies, waits for them, and re-layouts  1.94 us (3%)
  between operations  0.65 us (1%)
    pallas_call x1, Pallas kernels, local(): pl.pallas_call(functools.partial(kernel, list(scratch)), out_shape=(jax.S...  58.3 us
    unnamed x4, local copies, waits for them, and re-layouts  1.94 us

profile of v4, /device:TPU:0, one launch (start us, length us, event | category | flops | bytes accessed | tf_op | source)
XLA Modules:
  0.0 60.9 jit_solution(7341619980658514762)
XLA Ops:
  0.6 58.3 %shard_map.104 = (f32[2,16,128]{2,1,0:T(8,128)}, f32[2,16,16]{2,1,0:T(8,128)}) custom-call(bf16[2,32,6144]{2,1,0:T(8,128)(2,1)} %g_ref.1, f32[512,128]{1,0:T(8,128)} %bitcast.2, f32[16,128]{1,0:T(8,128)} %en_ref.1, s32[16,128]{1,0:T(8,128)} %mask_ref.1, s32[3,1024]{1,0:T(4,128)} %lat_ref.1, s32[2,128]{1,0:T(2,128)} %kq_ref.1, s32[1,128]{1,0:T(1,128)} %bitcast.3, ...), custom_call_target="tpu_custom_call" | custom-call | tf_op jit(solution)/shard_map/pallas_call | solution.py:489
  59.0 0.0 copy-start
  59.0 1.3 %copy.13 = f32[2,16,128]{2,1,0:T(8,128)} copy(f32[2,16,128]{2,1,0:T(8,128)} %get-tuple-element.4) | data formatting | bytes 32768
  60.3 0.0 copy-done
  60.3 0.6 copy.14
Async XLA Ops:
  59.0 1.3 %copy-start = (f32[2,16,16]{2,1,0:T(8,128)S(1)}, f32[2,16,16]{2,1,0:T(8,128)}, u32[]{:S(2)}) copy-start(f32[2,16,16]{2,1,0:T(8,128)} %get-tuple-element.5) | copy-start | bytes 6148

commit v5 on v4

--- a/solution.py
+++ b/solution.py
@@ -153,24 +153,23 @@
     lax.fori_loop(0, 8, pair, 0)
 
 
-def partner_set(s, step):
-    return s // 4 * 4 + lax.rem(lax.rem(s, 4) + step + 1, 4)
-
-
-def levels(r, s, step):
-    own = pieces(r.e[s, 0:16], 3)
-    far = partner_set(s, step)
-    far_e = pieces(r.e[far, 0:16], 3) + [r.e[far, 16:32].astype(BF16)]
-    moved = dot_nt(jnp.concatenate(far_e, 0), r.perm[...]).astype(BF16)
+def partner_of(slot, step):
+    return slot // 4 * 4 + lax.rem(lax.rem(slot, 4) + 7 - step, 4)
+
+
+def levels(r, slot, step):
+    own = pieces(r.e[slot, 0:16], 3)
+    moved = dot_nt(jnp.concatenate(own + [r.e[slot, 16:32].astype(BF16)], 0), r.perm[...]).astype(BF16)
     yield
     both = dot(jnp.concatenate(own + [moved], 0), r.rep[...])
     yield
-    r.ex[pl.ds(pl.multiple_of(s * 16, 16), 16)] = both[0:16] + both[16:32] + both[32:48]
+    r.ex[pl.ds(pl.multiple_of(slot * 16, 16), 16)] = both[0:16] + both[16:32] + both[32:48]
     pick = iota((16, 2048), 0) == iota((16, 2048), 1) % 16
     fe = jnp.where(pick, both[48:64] + both[64:80] + both[80:96], 0.0).sum(0, keepdims=True)
     fm = jnp.where(pick, both[96:112], 0.0).sum(0, keepdims=True)
     occ = 1.0 / (jnp.exp(fe * (1.0 / KT)) + 1.0)
-    r.fa[pl.ds(pl.multiple_of(s * 8, 8), 8)] = jnp.concatenate([fe, fm, occ, jnp.zeros((5, 2048), F32)], 0)
+    rows = pl.ds(pl.multiple_of(partner_of(slot, step) * 8, 8), 8)
+    r.fa[rows] = jnp.concatenate([fe, fm, occ, jnp.zeros((5, 2048), F32)], 0)
 
 
 def regroup_columns(tiles):
@@ -188,9 +187,9 @@
     return dot(r.mix[...], regroup_columns(tiles)).astype(BF16)
 
 
-def rotations(r, w, s, step):
-    left, at = (r.eye[...], s) if w == 0 else (r.turned[...], partner_set(s, step))
-    points = dot_nt(left, r.u[at]).astype(BF16)
+def rotations(r, w, slot, step):
+    left, s = (r.eye[...], slot) if w == 0 else (r.turned[...], partner_of(slot, step))
+    points = dot_nt(left, r.u[slot]).astype(BF16)
     yield
     cols = regroup_columns([[points[:, c * 256 + hi * 128:c * 256 + hi * 128 + 128] for hi in range(2)]
                             for c in range(2)])
@@ -317,7 +316,7 @@
     dma = pltpu.SemaphoreType.DMA
     return dict(
         in_sem=dma((8,)), near_sem=dma((1,)), z_sem=dma((2,)), p_sem=dma((2,)), g_send=dma((1,)), g_recv=dma((3,)),
-        u_send=dma((1,)), u_recv=dma((4,)), e_send=dma((1,)), e_recv=dma((4,)), a_sem=dma((2,)), b_sem=dma((2,)),
+        u_send=dma((1,)), u_recv=dma((8,)), e_send=dma((1,)), e_recv=dma((8,)), a_sem=dma((2,)), b_sem=dma((2,)),
     )
 
 
@@ -378,6 +377,10 @@
         for hop in (1, 3, 2):
             remote(piece, piece, r.p_sem.at[0], r.p_sem.at[1], plane(hop, c == 0)).start()
 
+    total(r.g.at[:, :, x, zh, y], r.near_sem.at[0])
+    for c in range(2):
+        first_leg(c, zh)
+
     chip, sibling = mine // 2, at(g // 2 * 2 + 1 - g % 2, x, zh, y)
 
     def share(slot, sem, device):
@@ -394,22 +397,16 @@
     r.e[mine, 0:16] = r.en[...]
     r.e[mine, 16:32] = r.mask[...].astype(F32)
     for hop in (1, 3, 2):
-        there = (chip + hop) % 4
-        share(mine, hop, at(there % 2 * 2 + g % 2, x, there // 2, y))
+        to = (chip + hop) % 4
+        share(mine, hop, at(to % 2 * 2 + g % 2, x, to // 2, y))
     share(mine, 0, sibling)
 
-    total(r.g.at[:, :, x, zh, y], r.near_sem.at[0])
-    for c in range(2):
-        first_leg(c, zh)
     constants(r)
     loads[4].wait()
     partner_order(r, r.kq[...], step)
-    loads[3].wait()
-    tables(r, r.lat[...], first)
     total(r.g.at[:, :, x, pz, y], r.z_sem.at[1])
     for c in range(2):
         first_leg(c, 1 - zh)
-    loop(lambda s: phases(r, s, first))
 
     def second_leg(m, c, hop):
         xs, ys = ((x + 4 - hop) % 4, y) if c == 0 else (x, (y + 4 - hop) % 4)
@@ -417,20 +414,38 @@
         for to in (1, 3, 2):
             remote(piece, piece, r.g_send.at[0], r.g_recv.at[m], plane(to, c == 1)).start()
 
+    for c in range(2):
+        second_leg(0, c, 0)
+    loads[3].wait()
+    tables(r, r.lat[...], first)
+    total(r.g.at[:, :, 0:3, :, 0], r.p_sem.at[1])
     for m in range(3):
         for hop in (0, 1, 3, 2):
             for c in range(2):
-                if m == 0 and hop == 1 and c == 0:
-                    total(r.g.at[:, :, 0:3, :, 0], r.p_sem.at[1])
-                second_leg(m, c, hop)
-
-    for hop in (1, 3, 2):
-        shared((chip + 4 - hop) % 4 * 2 + g % 2, hop)
-        share((chip + 4 - hop) % 4 * 2 + g % 2, 0, sibling)
-    total(r.u.at[0:4], r.u_recv.at[0])
-    total(r.e.at[0:4], r.e_recv.at[0])
-    loop(lambda i: together([levels(r, i * 4 + q, step) for q in range(4)]), 2)
-    loop(lambda i: together([rotations(r, w, i * 4 + q, step) for q in range(4) for w in range(2)]), 2)
+                if m or hop:
+                    second_leg(m, c, hop)
+    loop(lambda s: phases(r, s, first))
+
+    def there(hop):
+        return (chip + 4 - hop) % 4
+
+    def forward(hop):
+        shared(there(hop) * 2 + g % 2, hop)
+        share(there(hop) * 2 + g % 2, 4 + hop, sibling)
+
+    def prepare(hop):
+        shared(there(hop) * 2 + 1 - g % 2, 4 + hop if hop else 0)
+        slots = [there(hop) * 2, there(hop) * 2 + 1]
+        together([rotations(r, w, slot, step) for slot in slots for w in range(2)]
+                 + [levels(r, slot, step) for slot in slots])
+
+    forward(1)
+    prepare(0)
+    forward(3)
+    forward(2)
+    prepare(1)
+    prepare(3)
+    prepare(2)
     loads[6].wait()
     loads[7].wait()
     onsite, phonon, bose = mode_terms(r.freq[...], r.froh[...], step, mode0)
@@ -486,7 +501,7 @@
     anywhere = pl.BlockSpec(memory_space=pl.ANY)
     vm = pl.BlockSpec(memory_space=pltpu.VMEM)
     scratch = {**scratch_shapes(), **io_shapes(), **semaphores()}
-    return pl.pallas_call(
+    results = pl.pallas_call(
         functools.partial(kernel, list(scratch)),
         out_shape=(jax.ShapeDtypeStruct((2, 16, 128), F32), jax.ShapeDtypeStruct((2, 16, 16), F32)),
         in_specs=[anywhere] * 9,
@@ -495,6 +510,18 @@
         compiler_params=pltpu.CompilerParams(collective_id=0, has_side_effects=True,
                                              vmem_limit_bytes=60 * 2 ** 20),
     )(g_real, u_rot.reshape(512, 128), energy, band_mask, lattice, kq_index, irr_id.reshape(1, 128), freq, froh)
+
+
+    def hand_over(sigma_ref, star_ref, sigma_out, star_out):
+        sigma_out[...] = sigma_ref[...]
+        star_out[...] = star_ref[...]
+
+    return pl.pallas_call(
+        hand_over,
+        out_shape=(jax.ShapeDtypeStruct((2, 16, 128), F32), jax.ShapeDtypeStruct((2, 16, 16), F32)),
+        in_specs=[vm, vm],
+        out_specs=(vm, vm),
+    )(*results)
 
 
 def solution(mesh):

time: 61.1 us -> 60.7 us (level)
  local copies, waits for them, and re-layouts: 1.94 us -> 0 us
  Pallas kernels: 58.3 us -> 59.9 us
    unnamed x4 -> x0, local copies, waits for them, and re-layouts: 1.94 us -> none
    pallas_call x0 -> x1, Pallas kernels: none -> 1.35 us  [local(): pl.pallas_call(hand_over, out_shape=(jax.ShapeDtypeStruct((2, 16, 128), F...]
where the time goes in v5:
time: 60.7 us; the launch traced here: 60.5 us
  Pallas kernels  59.9 us (99%)
  between operations  0.64 us (1%)
    pallas_call x1, Pallas kernels, local(): pl.pallas_call(functools.partial(kernel, list(scratch)), out_shape=(jax.S...  58.6 us
    pallas_call x1, Pallas kernels, local(): pl.pallas_call(hand_over, out_shape=(jax.ShapeDtypeStruct((2, 16, 128), F...  1.35 us

profile of v5, /device:TPU:0, one launch (start us, length us, event | category | flops | bytes accessed | tf_op | source)
XLA Modules:
  0.0 60.5 jit_solution(4263399785738322774)
XLA Ops:
  0.6 58.6 %shard_map.104 = (f32[2,16,128]{2,1,0:T(8,128)}, f32[2,16,16]{2,1,0:T(8,128)}) custom-call(bf16[2,32,6144]{2,1,0:T(8,128)(2,1)} %g_ref.1, f32[512,128]{1,0:T(8,128)} %bitcast.2, f32[16,128]{1,0:T(8,128)} %en_ref.1, s32[16,128]{1,0:T(8,128)} %mask_ref.1, s32[3,1024]{1,0:T(4,128)} %lat_ref.1, s32[2,128]{1,0:T(2,128)} %kq_ref.1, s32[1,128]{1,0:T(1,128)} %bitcast.3, ...), custom_call_target="tpu_custom_call" | custom-call | tf_op jit(solution)/shard_map/pallas_call | solution.py:504
  59.2 1.3 %shard_map.105 = (f32[2,16,128]{2,1,0:T(8,128)}, f32[2,16,16]{2,1,0:T(8,128)}) custom-call(f32[2,16,128]{2,1,0:T(8,128)} %get-tuple-element.4.sigma_ref, f32[2,16,16]{2,1,0:T(8,128)} %get-tuple-element.5.star_ref), custom_call_target="tpu_custom_call" | custom-call | tf_op jit(solution)/shard_map/pallas_call | solution.py:519

commit v6 on v5

--- a/solution.py
+++ b/solution.py
@@ -266,8 +266,8 @@
         r.sums[pl.ds(pl.multiple_of(s * 32 + 16, 16), 16), cols] = im * (-ETA)
 
 
-def band_sum(r):
-    hi, lo = pieces(r.sums[...], 2)
+def band_sum(r, half):
+    hi, lo = pieces(r.sums[half * 128:half * 128 + 128], 2)
     return (dot(hi, r.rept[...]) + dot(lo, r.rept[...])) * (1.0 / 384.0)
 
 
@@ -411,7 +411,7 @@
     def second_leg(m, c, hop):
         xs, ys = ((x + 4 - hop) % 4, y) if c == 0 else (x, (y + 4 - hop) % 4)
         piece = r.g.at[m, c, xs, :, ys]
-        for to in (1, 3, 2):
+        for to in (2, 1, 3):
             remote(piece, piece, r.g_send.at[0], r.g_recv.at[m], plane(to, c == 1)).start()
 
     for c in range(2):
@@ -458,19 +458,31 @@
         vertex(r, m, 1, onsite[m])
         regroup_vertex(r, m, 0)
     regroup_vertex(r, 2, 1)
-    loop(lambda i: together([self_energy(r, 2 * i + q, q, bose, phonon) for q in range(2)]), 4)
-    sums = band_sum(r)
-    for s in range(8):
-        r.part[s] = sums[s * 32:s * 32 + 32]
-
-    for hop, g2, zh2 in column(g, zh):
-        remote(r.part.at[zh2 * 4 + g2], r.got.at[hop], r.a_sem.at[0], r.a_sem.at[1], at(g2, x, zh2, y)).start()
+    def sums_of(half):
+        sums = band_sum(r, half)
+        for s in range(4):
+            r.part[half * 4 + s] = sums[s * 32:s * 32 + 32]
+
+    def to_owners(z):
+        for g2 in range(4):
+            slot = z * 4 + g2
+            copy = remote(r.part.at[slot], r.got.at[mine], r.a_sem.at[0], r.a_sem.at[1], (g2, x * 8 + z * 4 + y))
+            pl.when(slot != mine)(copy.start)
+
+    loop(lambda i: together([self_energy(r, 2 * i + q, q, bose, phonon) for q in range(2)]), 2)
+    sums_of(0)
+    to_owners(0)
+    loop(lambda i: together([self_energy(r, 2 * i + q + 4, q, bose, phonon) for q in range(2)]), 2)
+    sums_of(1)
+    to_owners(1)
+
     loads[5].wait()
     member = jnp.where(iota((512, 128), 0) == r.irr[...], 1.0, 0.0).astype(BF16)
     total(r.got.at[1:8], r.a_sem.at[1])
-    sigma = r.part[mine]
-    for hop in range(1, 8):
-        sigma = sigma + r.got[hop]
+    r.got[mine] = r.part[mine]
+    sigma = r.got[0]
+    for slot in range(1, 8):
+        sigma = sigma + r.got[slot]
     sigma_ref[0] = sigma[0:16]
     sigma_ref[1] = sigma[16:32]
     columns = jnp.concatenate(pieces(sigma, 3) + [jnp.ones((32, 128), BF16)], 0)

time: 60.7 us -> 60.2 us (level)
  no operation moved by 1% of the time
where the time goes in v6:
time: 60.2 us; the launch traced here: 60 us
  Pallas kernels  59.4 us (99%)
  between operations  0.64 us (1%)
    pallas_call x1, Pallas kernels, local(): pl.pallas_call(functools.partial(kernel, list(scratch)), out_shape=(jax.S...  58 us
    pallas_call x1, Pallas kernels, local(): pl.pallas_call(hand_over, out_shape=(jax.ShapeDtypeStruct((2, 16, 128), F...  1.35 us

profile of v6, /device:TPU:0, one launch (start us, length us, event | category | flops | bytes accessed | tf_op | source)
XLA Modules:
  0.0 60.0 jit_solution(751180117442965100)
XLA Ops:
  0.6 58.0 %shard_map.104 = (f32[2,16,128]{2,1,0:T(8,128)}, f32[2,16,16]{2,1,0:T(8,128)}) custom-call(bf16[2,32,6144]{2,1,0:T(8,128)(2,1)} %g_ref.1, f32[512,128]{1,0:T(8,128)} %bitcast.2, f32[16,128]{1,0:T(8,128)} %en_ref.1, s32[16,128]{1,0:T(8,128)} %mask_ref.1, s32[3,1024]{1,0:T(4,128)} %lat_ref.1, s32[2,128]{1,0:T(2,128)} %kq_ref.1, s32[1,128]{1,0:T(1,128)} %bitcast.3, ...), custom_call_target="tpu_custom_call" | custom-call | tf_op jit(solution)/shard_map/pallas_call | solution.py:516
  58.7 1.3 %shard_map.105 = (f32[2,16,128]{2,1,0:T(8,128)}, f32[2,16,16]{2,1,0:T(8,128)}) custom-call(f32[2,16,128]{2,1,0:T(8,128)} %get-tuple-element.4.sigma_ref, f32[2,16,16]{2,1,0:T(8,128)} %get-tuple-element.5.star_ref), custom_call_target="tpu_custom_call" | custom-call | tf_op jit(solution)/shard_map/pallas_call | solution.py:531
